TPU v7x, 32 devices: a whole 2x2x4 slice. The times are simulated.
32 devices in a mesh: wide: 16 (over z, x, core), heads: 2 (over y).
Axes of the slice: x: 2, y: 2, z: 4, core: 2. Of those that a mesh axis runs over, the one named last changes fastest.
Arguments:
- inputs: bfloat16 [32768, 1280], P('wide'), may hold values from -6 to 6
- segment_ids: int32 [32768], P('wide'), may hold values from 0 to 4095, never falling along the last dimension, each value on 1 to 16 neighbouring positions
- cotangent: bfloat16 [32768, 1280], P('wide'), may hold values from -6 to 6
- w_query: bfloat16 [1280, 1280], P('wide', 'heads'), may hold values from -0.15625 to 0.15625
- w_key: bfloat16 [1280, 1280], P('wide', 'heads'), may hold values from -0.15625 to 0.15625
- w_value: bfloat16 [1280, 1280], P('wide', 'heads'), may hold values from -0.15625 to 0.15625
- w_out: bfloat16 [1280, 1280], P('heads', 'wide'), may hold values from -0.3125 to 0.3125
- w_up: bfloat16 [1280, 1280], P('wide', 'heads'), may hold values from -0.15625 to 0.15625
- w_down: bfloat16 [1280, 1280], P('heads', 'wide'), may hold values from -0.25 to 0.25
- b_query: float32 [1280], replicated, may hold values from -3 to 3
- b_value: float32 [1280], replicated, may hold values from -3 to 3
- b_out: float32 [1280], replicated, may hold values from -3 to 3
- b_up: float32 [1280], replicated, may hold values from -3 to 3
- b_down: float32 [1280], replicated, may hold values from -3 to 3
- dim_scale: float32 [80], replicated, may hold values from -1 to 1.5
- gain_attn: float32 [1280], replicated, may hold values from 0.5 to 1.5
- gain_mlp: float32 [1280], replicated, may hold values from 0.5 to 1.5
Outputs:
- output: bfloat16 [32768, 1280], P(('wide', 'heads'))
- input_grad: float32 [32768, 1280], P(('wide', 'heads'))
- grad_w_query: float32 [1280, 1280], P('wide', 'heads')
- grad_w_key: float32 [1280, 1280], P('wide', 'heads')
- grad_w_value: float32 [1280, 1280], P('wide', 'heads')
- grad_w_out: float32 [1280, 1280], P('heads', 'wide')
- grad_w_up: float32 [1280, 1280], P('wide', 'heads')
- grad_w_down: float32 [1280, 1280], P('heads', 'wide')
- grad_b_query: float32 [1280], replicated
- grad_b_value: float32 [1280], replicated
- grad_b_out: float32 [1280], replicated
- grad_b_up: float32 [1280], replicated
- grad_b_down: float32 [1280], replicated
- grad_dim_scale: float32 [80], replicated
- grad_gain_attn: float32 [1280], replicated
- grad_gain_mlp: float32 [1280], replicated
Inputs may be any that keep to these rules, and one draw needn't show every extreme that they name: `segment_ids`: segment numbers never fall along the tokens; a segment has 1 to 16 tokens.
All inputs are finite; a program needn't handle non-finite values.
Results may differ from a plain program's by a relative error of at most 0.015.
Values may be sent and summed in bfloat16 or wider, within the bound.
A program may use at most 192 MiB of HBM per device.

v0:
```python
import math

import jax
import jax.numpy as jnp
from jax import lax
from jax.sharding import PartitionSpec as P

DH = 80
PATCHES = 16


eps = 1e-06
query_base = 1.442695041


def dot_plain(left, right):
    return jnp.dot(left, right, preferred_element_type=jnp.float32)


def dot_left(left, right):
    return lax.dot_general(
        left, right, (((0,), (0,)), ((), ())), preferred_element_type=jnp.float32
    )


def dot_right(left, right):
    return lax.dot_general(
        left, right, (((1,), (1,)), ((), ())), preferred_element_type=jnp.float32
    )


def inverse_rms(values):
    return lax.rsqrt(jnp.mean(values * values, axis=-1, keepdims=True) + eps)


def norm_back(values, gain_vec, grad_in):
    factor = inverse_rms(values)
    inner = jnp.mean(grad_in * gain_vec * values, axis=-1, keepdims=True)
    grad_out = factor * gain_vec * grad_in - values * factor * factor * factor * inner
    return (grad_out, jnp.sum(grad_in * values * factor, axis=0))


def tile_mask(seg_tiles, tile_len):
    position = jnp.arange(tile_len)
    same_row = position[:, None] // PATCHES == position[None, :] // PATCHES
    causal = position[:, None] >= position[None, :]
    same_seg = seg_tiles[:, :, None] == seg_tiles[:, None, :]
    return (same_seg & (same_row & causal)[None])[:, None]


def masked_scores(query_tiles, key_tiles, allowed):
    scores = jnp.einsum(
        "bqhe,bkhe->bhqk", query_tiles, key_tiles, preferred_element_type=jnp.float32
    )
    return jnp.where(allowed, scores, -1e30)


def place_part(vector, length, offset):
    return lax.dynamic_update_slice_in_dim(jnp.zeros((length,), jnp.float32), vector, offset, 0)


def shards(
    inputs,
    segment_ids,
    cotangent,
    w_query,
    w_key,
    w_value,
    w_out,
    w_up,
    w_down,
    b_query,
    b_value,
    b_out,
    b_up,
    b_down,
    dim_scale,
    gain_attn,
    gain_mlp,
):
    tok_rows = inputs.shape[0]
    head_groups = lax.axis_size("heads")
    head_index = lax.axis_index("heads")
    half_rows = tok_rows // head_groups
    local_hd = w_query.shape[1]
    local_ff = w_up.shape[1]
    local_heads = local_hd // DH
    tile_len = min(128, tok_rows)
    tile_count = tok_rows // tile_len
    row_start = head_index * half_rows
    input_full = inputs.astype(jnp.float32)
    input_half = lax.dynamic_slice_in_dim(input_full, row_start, half_rows, 0)
    cot_half = lax.dynamic_slice_in_dim(cotangent, row_start, half_rows, 0)
    grad_half = cot_half.astype(jnp.float32)
    bias_query = lax.dynamic_slice_in_dim(b_query, head_index * local_hd, local_hd, 0)
    bias_value = lax.dynamic_slice_in_dim(b_value, head_index * local_hd, local_hd, 0)
    bias_up = lax.dynamic_slice_in_dim(b_up, head_index * local_ff, local_ff, 0)
    scale_const = query_base / math.sqrt(DH)
    query_scale = scale_const * jax.nn.softplus(dim_scale)
    tile_shape = (tile_count, tile_len, local_heads, DH)
    query_full, key_full, value_full, out_full = (
        lax.all_gather(w_query, "wide", axis=0, tiled=True),
        lax.all_gather(w_key, "wide", axis=0, tiled=True),
        lax.all_gather(w_value, "wide", axis=0, tiled=True),
        lax.all_gather(w_out, "wide", axis=1, tiled=True),
    )
    normed_one = (input_full * inverse_rms(input_full) * gain_attn).astype(jnp.bfloat16)
    query_proj = dot_plain(normed_one, query_full) + bias_query
    query_tiles = (query_proj.reshape(tile_shape) * query_scale).astype(jnp.bfloat16)
    key_tiles = dot_plain(normed_one, key_full).astype(jnp.bfloat16).reshape(tile_shape)
    value_tiles = (
        (dot_plain(normed_one, value_full) + bias_value).astype(jnp.bfloat16).reshape(tile_shape)
    )
    allowed = tile_mask(segment_ids.reshape(tile_count, tile_len), tile_len)
    scores = masked_scores(query_tiles, key_tiles, allowed)
    row_max = jnp.max(scores, axis=-1, keepdims=True)
    exp_scores = jnp.exp(scores - row_max)
    row_total = jnp.sum(exp_scores, axis=-1, keepdims=True)
    attn_probs = exp_scores / row_total
    log_total = row_max + jnp.log(row_total)
    attended = jnp.einsum(
        "bhqk,bkhe->bqhe",
        attn_probs.astype(jnp.bfloat16),
        value_tiles,
        preferred_element_type=jnp.float32,
    )
    attended = attended.reshape(tok_rows, local_hd).astype(jnp.bfloat16)
    up_full, down_full = (
        lax.all_gather(w_up, "wide", axis=0, tiled=True),
        lax.all_gather(w_down, "wide", axis=1, tiled=True),
    )
    attn_half = lax.psum_scatter(
        dot_plain(attended, out_full), "heads", scatter_dimension=0, tiled=True
    )
    residual = input_half + attn_half + b_out
    normed_half = (residual * inverse_rms(residual) * gain_mlp).astype(jnp.bfloat16)
    normed_two = lax.all_gather(normed_half, "heads", axis=0, tiled=True)
    up_proj = dot_plain(normed_two, up_full) + bias_up
    activated = jax.nn.gelu(up_proj).astype(jnp.bfloat16)
    mlp_half = lax.psum_scatter(
        dot_plain(activated, down_full).astype(jnp.bfloat16),
        "heads",
        scatter_dimension=0,
        tiled=True,
    ).astype(jnp.float32)
    output = (residual + mlp_half + b_down).astype(jnp.bfloat16)
    up_full, down_full = (
        lax.all_gather(w_up, "wide", axis=0, tiled=True),
        lax.all_gather(w_down, "wide", axis=1, tiled=True),
    )
    grad_down = dot_left(activated, cotangent)
    grad_act = dot_right(cotangent, down_full)
    unused_value, gelu_pull = jax.vjp(jax.nn.gelu, up_proj)
    grad_up_proj = gelu_pull(grad_act)[0].astype(jnp.bfloat16)
    grad_up = dot_left(normed_two, grad_up_proj)
    bias_up_term = place_part(
        jnp.sum(grad_up_proj.astype(jnp.float32), axis=0), b_up.shape[0], head_index * local_ff
    )
    grad_norm_two = lax.psum_scatter(
        dot_right(grad_up_proj, up_full).astype(jnp.bfloat16),
        "heads",
        scatter_dimension=0,
        tiled=True,
    ).astype(jnp.float32)
    back_two, grad_gain_two = norm_back(residual, gain_mlp, grad_norm_two)
    grad_resid = grad_half + back_two
    branch_half = grad_resid.astype(jnp.bfloat16)
    query_full, key_full, value_full, out_full = (
        lax.all_gather(w_query, "wide", axis=0, tiled=True),
        lax.all_gather(w_key, "wide", axis=0, tiled=True),
        lax.all_gather(w_value, "wide", axis=0, tiled=True),
        lax.all_gather(w_out, "wide", axis=1, tiled=True),
    )
    grad_branch = lax.all_gather(branch_half, "heads", axis=0, tiled=True)
    grad_out = dot_left(attended, grad_branch)
    grad_attended = dot_right(grad_branch, out_full).astype(jnp.bfloat16).reshape(tile_shape)
    probs_again = jnp.exp(masked_scores(query_tiles, key_tiles, allowed) - log_total)
    grad_probs = jnp.einsum(
        "bqhe,bkhe->bhqk", grad_attended, value_tiles, preferred_element_type=jnp.float32
    )
    inner = jnp.sum(probs_again * grad_probs, axis=-1, keepdims=True)
    grad_scores = (probs_again * (grad_probs - inner)).astype(jnp.bfloat16)
    grad_qs = jnp.einsum(
        "bhqk,bkhe->bqhe", grad_scores, key_tiles, preferred_element_type=jnp.float32
    )
    grad_key_proj = jnp.einsum(
        "bhqk,bqhe->bkhe", grad_scores, query_tiles, preferred_element_type=jnp.float32
    )
    grad_key_proj = grad_key_proj.reshape(tok_rows, local_hd).astype(jnp.bfloat16)
    grad_value_proj = jnp.einsum(
        "bhqk,bqhe->bkhe",
        probs_again.astype(jnp.bfloat16),
        grad_attended,
        preferred_element_type=jnp.float32,
    )
    grad_value_proj = grad_value_proj.reshape(tok_rows, local_hd).astype(jnp.bfloat16)
    grad_dim = (
        jnp.sum(grad_qs * query_proj.reshape(tile_shape), axis=(0, 1, 2))
        * scale_const
        * jax.nn.sigmoid(dim_scale)
    )
    grad_query_proj = (grad_qs * query_scale).reshape(tok_rows, local_hd).astype(jnp.bfloat16)
    grad_query = dot_left(normed_one, grad_query_proj)
    grad_key = dot_left(normed_one, grad_key_proj)
    grad_value = dot_left(normed_one, grad_value_proj)
    sum_query = jnp.sum(grad_query_proj.astype(jnp.float32), axis=0)
    sum_value = jnp.sum(grad_value_proj.astype(jnp.float32), axis=0)
    norm_terms = (
        dot_right(grad_query_proj, query_full)
        + dot_right(grad_key_proj, key_full)
        + dot_right(grad_value_proj, value_full)
    )
    grad_norm_one = lax.psum_scatter(
        norm_terms.astype(jnp.bfloat16), "heads", scatter_dimension=0, tiled=True
    ).astype(jnp.float32)
    back_one, grad_gain_one = norm_back(input_half, gain_attn, grad_norm_one)
    input_grad = grad_resid + back_one
    grad_up_w, grad_down_w = (
        lax.psum_scatter(grad_up, "wide", scatter_dimension=0, tiled=True),
        lax.psum_scatter(grad_down, "wide", scatter_dimension=1, tiled=True),
    )
    grad_query_w, grad_key_w, grad_value_w, grad_out_w = (
        lax.psum_scatter(grad_query, "wide", scatter_dimension=0, tiled=True),
        lax.psum_scatter(grad_key, "wide", scatter_dimension=0, tiled=True),
        lax.psum_scatter(grad_value, "wide", scatter_dimension=0, tiled=True),
        lax.psum_scatter(grad_out, "wide", scatter_dimension=1, tiled=True),
    )
    small_sums = lax.psum(
        (
            grad_gain_one,
            grad_gain_two,
            jnp.sum(grad_resid, axis=0),
            jnp.sum(grad_half, axis=0),
            grad_dim,
            place_part(sum_query, b_query.shape[0], head_index * local_hd),
            place_part(sum_value, b_value.shape[0], head_index * local_hd),
            bias_up_term,
        ),
        ("wide", "heads"),
    )
    (
        gain_one_sum,
        gain_two_sum,
        bias_out_sum,
        bias_down_sum,
        dim_sum,
        bias_query_sum,
        bias_value_sum,
        bias_up_sum,
    ) = small_sums
    return (
        output,
        input_grad,
        grad_query_w,
        grad_key_w,
        grad_value_w,
        grad_out_w,
        grad_up_w,
        grad_down_w,
        bias_query_sum,
        bias_value_sum,
        bias_out_sum,
        bias_up_sum,
        bias_down_sum,
        dim_sum,
        gain_one_sum,
        gain_two_sum,
    )


def solution(mesh):
    return jax.shard_map(
        shards,
        mesh=mesh,
        in_specs=(
            P("wide", None),
            P("wide"),
            P("wide", None),
            P("wide", "heads"),
            P("wide", "heads"),
            P("wide", "heads"),
            P("heads", "wide"),
            P("wide", "heads"),
            P("heads", "wide"),
            P(),
            P(),
            P(),
            P(),
            P(),
            P(),
            P(),
            P(),
        ),
        out_specs=(
            P(("wide", "heads"), None),
            P(("wide", "heads"), None),
            P("wide", "heads"),
            P("wide", "heads"),
            P("wide", "heads"),
            P("heads", "wide"),
            P("wide", "heads"),
            P("heads", "wide"),
            P(),
            P(),
            P(),
            P(),
            P(),
            P(),
            P(),
            P(),
        ),
        check_vma=False,
    )
```

profile of v0, /device:TPU:0, one launch (start us, length us, event | category | flops | bytes accessed | tf_op | source)
XLA Modules:
  0.0 1288.0 jit_solution(7532887947847363733)
XLA Ops:
  12.3 3.6 multiply_reduce_fusion
  16.3 36.5 %all-gather.9.cloned.1.call-done = bf16[1280,640]{1,0:T(8,128)(2,1)} async-done(((bf16[80,640]{1,0:T(8,128)(2,1)}), bf16[1280,640]{1,0:T(8,128)(2,1)}) %all-gather.9.cloned.1.call-update) | async-done | bytes 1638416 | tf_op jit(solution)/shard_map/all_gather | solution.py:104
  52.9 7.4 add_convert_fusion.2
  60.2 33.6 %all-gather.11.cloned.1.call-done = bf16[1280,640]{1,0:T(8,128)(2,1)} async-done(((bf16[80,640]{1,0:T(8,128)(2,1)}), bf16[1280,640]{1,0:T(8,128)(2,1)}) %all-gather.11.cloned.1.call-update) | async-done | bytes 1638416 | tf_op jit(solution)/shard_map/all_gather | solution.py:102
  93.9 9.7 convolution_add_fusion
  103.5 31.4 %all-gather.13.cloned.1.call-done = bf16[1280,640]{1,0:T(8,128)(2,1)} async-done(((bf16[80,640]{1,0:T(8,128)(2,1)}), bf16[1280,640]{1,0:T(8,128)(2,1)}) %all-gather.13.cloned.1.call-update) | async-done | bytes 1638416 | tf_op jit(solution)/shard_map/all_gather | solution.py:103
  134.9 9.0 convolution_convert_fusion.3
  143.9 5.2 reshape.228
  149.1 6.3 copy.50
  155.4 5.2 reshape.230
  160.6 6.1 copy.49
  166.7 9.4 reshape.229
  176.1 8.3 copy.47
  184.4 4.5 select_reduce_fusion
  188.9 2.4 fusion
  192.5 2.4 convert_bitcast_fusion.1
  196.7 10.0 fusion.42
  207.4 7.6 convert_element_type.111
  215.0 112.7 %reduce-scatter.11.cloned.1.call-done = f32[1024,1280]{1,0:T(8,128)} async-done(((f32[2048,1280]{1,0:T(8,128)}), f32[1024,1280]{1,0:T(8,128)}) %reduce-scatter.11.cloned.1.call-update) | async-done | bytes 5242896 | tf_op jit(solution)/shard_map/reduce_scatter | solution.py:132
  327.7 5.8 multiply_reduce_fusion.3
  333.5 2.3 copy-done.1
  335.8 2.0 multiply_convert_fusion.3
  338.7 30.9 %all-gather.19.cloned.1.call-done = bf16[1280,640]{1,0:T(8,128)(2,1)} async-done(((bf16[80,640]{1,0:T(8,128)(2,1)}), bf16[1280,640]{1,0:T(8,128)(2,1)}) %all-gather.19.cloned.1.call-update) | async-done | bytes 1638416 | tf_op jit(solution)/shard_map/all_gather | solution.py:129
  369.7 69.6 %all-gather.17.cloned.1.call-done = bf16[2048,1280]{1,0:T(8,128)(2,1)} async-done(((bf16[1024,1280]{1,0:T(8,128)(2,1)}), bf16[2048,1280]{1,0:T(8,128)(2,1)}) %all-gather.17.cloned.1.call-update) | async-done | bytes 5242896 | tf_op jit(solution)/shard_map/all_gather | solution.py:137
  439.3 9.5 fusion.64
  448.8 32.6 %all-gather.21.cloned.1.call-done = bf16[640,1280]{0,1:T(8,128)(2,1)} async-done(((bf16[640,80]{0,1:T(8,128)(2,1)}), bf16[640,1280]{0,1:T(8,128)(2,1)}) %all-gather.21.cloned.1.call-update) | async-done | bytes 1638416 | tf_op jit(solution)/shard_map/all_gather | solution.py:130
  481.4 10.2 convert_reduce_fusion.1
  493.1 6.0 convolution_convert_fusion
  500.5 10.5 convolution_convert_fusion.1
  511.1 52.7 %reduce-scatter.15.cloned.1.call-done = bf16[1024,1280]{1,0:T(8,128)(2,1)} async-done(((bf16[2048,1280]{1,0:T(8,128)(2,1)}), bf16[1024,1280]{1,0:T(8,128)(2,1)}) %reduce-scatter.15.cloned.1.call-update) | async-done | bytes 2621456 | tf_op jit(solution)/shard_map/reduce_scatter | solution.py:159
  563.9 5.0 fusion.13
  568.9 63.0 %reduce-scatter.13.cloned.1.call-done = bf16[1024,1280]{1,0:T(8,128)(2,1)} async-done(((bf16[2048,1280]{1,0:T(8,128)(2,1)}), bf16[1024,1280]{1,0:T(8,128)(2,1)}) %reduce-scatter.13.cloned.1.call-update) | async-done | bytes 2621456 | tf_op jit(solution)/shard_map/reduce_scatter | solution.py:140
  631.8 6.8 fusion.62
  638.7 2.4 copy-done.2
  641.1 1.8 convert_element_type.129
  643.2 68.5 %all-gather.23.cloned.1.call-done = bf16[2048,1280]{1,0:T(8,128)(2,1)} async-done(((bf16[1024,1280]{1,0:T(8,128)(2,1)}), bf16[2048,1280]{1,0:T(8,128)(2,1)}) %all-gather.23.cloned.1.call-update) | async-done | bytes 5242896 | tf_op jit(solution)/shard_map/all_gather | solution.py:174
  711.6 7.2 convolution_convert_fusion.2
  718.9 5.2 reshape.231
  724.1 6.1 copy.54
  730.2 8.0 convert_reduce_fusion.2
  738.3 10.1 multiply_reduce_fusion.1
  748.4 5.4 multiply_convert_fusion.1
  753.8 1.8 convert_reduce_fusion.3
  755.7 3.1 convert_bitcast_fusion
  758.7 1.7 copy.63
  763.9 7.8 fusion.34
  771.7 8.3 fusion.38
  780.0 11.3 add_convert_fusion
  791.4 9.4 fusion.65
  801.1 10.3 fusion.60
  811.4 9.2 fusion.40
  821.0 10.1 fusion.36
  831.2 9.8 fusion.32
  841.3 9.1 fusion.29
  851.5 5.7 reduce-scatter.17.cloned.1.call-done
  857.2 5.0 fusion.19
  862.2 41.1 %all-reduce = (f32[1280]{0:T(1024)}, f32[1280]{0:T(1024)}, f32[1280]{0:T(1024)}, f32[1280]{0:T(1024)}, f32[1280]{0:T(1024)}, /*index=5*/f32[80]{0:T(128)}, f32[1280]{0:T(1024)}, f32[1280]{0:T(1024)}) all-reduce(f32[1280]{0:T(1024)S(1)} %dynamic_update_slice.9, ...), channel_id=1, replica_groups=mesh['wide'=16,'heads'=2] {'wide','heads'}, use_global_device_ids=true, to_apply=%region_19.20 | all-reduce | flops 9040 | bytes 72320 | tf_op jit(solution)/shard_map/psum | solution.py:228
  903.3 6.5 fusion.15
  909.9 19.7 %reduce-scatter.27.cloned.1.call-done = f32[80,640]{1,0:T(8,128)} async-done(((f32[1280,640]{1,0:T(8,128)}), f32[80,640]{1,0:T(8,128)}) %reduce-scatter.27.cloned.1.call-update) | async-done | bytes 204816 | tf_op jit(solution)/shard_map/reduce_scatter | solution.py:219
  929.5 70.0 %reduce-scatter.29.cloned.1.call-done = f32[640,80]{0,1:T(8,128)} async-done(((f32[640,1280]{0,1:T(8,128)}), f32[640,80]{0,1:T(8,128)}) %reduce-scatter.29.cloned.1.call-update) | async-done | bytes 204816 | tf_op jit(solution)/shard_map/reduce_scatter | solution.py:220
  999.6 70.6 %reduce-scatter.25.cloned.1.call-done = f32[640,80]{0,1:T(8,128)} async-done(((f32[640,1280]{0,1:T(8,128)}), f32[640,80]{0,1:T(8,128)}) %reduce-scatter.25.cloned.1.call-update) | async-done | bytes 204816 | tf_op jit(solution)/shard_map/reduce_scatter | solution.py:226
  1070.1 70.0 %reduce-scatter.19.cloned.1.call-done = f32[80,640]{1,0:T(8,128)} async-done(((f32[1280,640]{1,0:T(8,128)}), f32[80,640]{1,0:T(8,128)}) %reduce-scatter.19.cloned.1.call-update) | async-done | bytes 204816 | tf_op jit(solution)/shard_map/reduce_scatter | solution.py:223
  1140.2 70.5 %reduce-scatter.21.cloned.1.call-done = f32[80,640]{1,0:T(8,128)} async-done(((f32[1280,640]{1,0:T(8,128)}), f32[80,640]{1,0:T(8,128)}) %reduce-scatter.21.cloned.1.call-update) | async-done | bytes 204816 | tf_op jit(solution)/shard_map/reduce_scatter | solution.py:224
  1210.7 70.1 %reduce-scatter.23.cloned.1.call-done = f32[80,640]{1,0:T(8,128)} async-done(((f32[1280,640]{1,0:T(8,128)}), f32[80,640]{1,0:T(8,128)}) %reduce-scatter.23.cloned.1.call-update) | async-done | bytes 204816 | tf_op jit(solution)/shard_map/reduce_scatter | solution.py:225
  (130 shorter events, 18.7 us)
Async XLA Ops:
  7.2 8.8 copy-start.17
  7.2 45.7 %copy-start.15 = (f32[1280]{0:T(1024)S(1)}, f32[1280]{0:T(1024)}, u32[]{:S(2)}) copy-start(f32[1280]{0:T(1024)} %param.32) | copy-start | bytes 15364
  7.2 45.7 %all-gather.9.cloned.1.call-start = ((), (), s32[]{:S(2)}) async-start(), calls=%async_computation.10 | async-start | bytes 1740800 | tf_op jit(solution)/shard_map/all_gather | solution.py:104
  7.9 85.9 %all-gather.11.cloned.1.call-start = ((), (), s32[]{:S(2)}) async-start(), calls=%async_computation.11 | async-start | bytes 1740800 | tf_op jit(solution)/shard_map/all_gather | solution.py:102
  8.7 126.2 %all-gather.13.cloned.1.call-start = ((), (), s32[]{:S(2)}) async-start(), calls=%async_computation.12 | async-start | bytes 1740800 | tf_op jit(solution)/shard_map/all_gather | solution.py:103
  9.4 187.3 %all-gather.15.cloned.1.call-start = ((), (), s32[]{:S(2)}) async-start(), calls=%async_computation.13 | async-start | bytes 1740800 | tf_op jit(solution)/shard_map/all_gather | solution.py:105
  10.0 317.7 %reduce-scatter.11.cloned.1.call-start = ((), (), s32[]{:S(2)}) async-start(), calls=%async_computation.14 | async-start | bytes 15728640 | tf_op jit(solution)/shard_map/reduce_scatter | solution.py:132
  15.9 119.0 %copy-start.21 = (f32[2048]{0:T(1024)}, f32[2048]{0:T(1024)S(1)}, u32[]{:S(2)}) copy-start(f32[2048]{0:T(1024)S(1)} %add_rsqrt_fusion) | copy-start | bytes 24580
  149.1 6.3 copy-start.12
  166.7 17.7 %copy-start.3 = (bf16[16,128,8,80]{1,3,2,0:T(8,128)(2,1)}, bf16[16,128,8,80]{1,3,2,0:T(8,128)(2,1)S(1)}, u32[]{:S(2)}) copy-start(bf16[16,128,8,80]{1,3,2,0:T(8,128)(2,1)S(1)} %copy.49) | copy-start | bytes 7864324
  188.8 6.1 copy-start
  188.8 3.7 copy-start.7
  196.7 10.1 copy-start.9
  206.8 162.9 %all-gather.19.cloned.1.call-start = ((), (), s32[]{:S(2)}) async-start(), calls=%async_computation.16 | async-start | bytes 1740800 | tf_op jit(solution)/shard_map/all_gather | solution.py:129
  207.3 120.3 %copy-start.19 = (f32[1280]{0:T(1024)S(1)}, f32[1280]{0:T(1024)}, u32[]{:S(2)}) copy-start(f32[1280]{0:T(1024)} %param.28) | copy-start | bytes 15364
  207.3 231.9 %all-gather.17.cloned.1.call-start = ((), (), s32[]{:S(2)}) async-start(), calls=%async_computation.15 | async-start | bytes 7864320 | tf_op jit(solution)/shard_map/all_gather | solution.py:137
  215.0 120.8 %copy-start.14 = (f32[1280]{0:T(1024)S(1)}, f32[1280]{0:T(1024)}, u32[]{:S(2)}) copy-start(f32[1280]{0:T(1024)} %param.33) | copy-start | bytes 15364
  333.5 2.3 copy-start.1
  335.8 2.8 copy-start.23
  337.8 143.6 %all-gather.21.cloned.1.call-start = ((), (), s32[]{:S(2)}) async-start(), calls=%async_computation.17 | async-start | bytes 1740800 | tf_op jit(solution)/shard_map/all_gather | solution.py:130
  338.6 225.3 %reduce-scatter.15.cloned.1.call-start = ((), (), s32[]{:S(2)}) async-start(), calls=%async_computation.19 | async-start | bytes 7864320 | tf_op jit(solution)/shard_map/reduce_scatter | solution.py:159
  448.8 44.3 %copy-start.26 = (bf16[1280,640]{1,0:T(8,128)(2,1)S(1)}, bf16[1280,640]{1,0:T(8,128)(2,1)}, u32[]{:S(2)}) copy-start(bf16[1280,640]{1,0:T(8,128)(2,1)} %all-gather.19.cloned.1.call-done) | copy-start | bytes 4915204
  491.6 1.5 copy-start.29
  499.1 1.4 copy-start.27
  499.1 132.7 %reduce-scatter.13.cloned.1.call-start = ((), (), s32[]{:S(2)}) async-start(), calls=%async_computation.18 | async-start | bytes 7864320 | tf_op jit(solution)/shard_map/reduce_scatter | solution.py:140
  511.1 120.8 %copy-start.20 = (f32[1280]{0:T(1024)S(1)}, f32[1280]{0:T(1024)}, u32[]{:S(2)}) copy-start(f32[1280]{0:T(1024)} %param.30) | copy-start | bytes 15364
  511.1 200.5 %all-gather.23.cloned.1.call-start = ((), (), s32[]{:S(2)}) async-start(), calls=%async_computation.20 | async-start | bytes 7864320 | tf_op jit(solution)/shard_map/all_gather | solution.py:174
  563.9 68.0 %copy-start.8 = (bf16[1024,1280]{1,0:T(8,128)(2,1)S(1)}, bf16[1024,1280]{1,0:T(8,128)(2,1)}, u32[]{:S(2)}) copy-start(bf16[1024,1280]{1,0:T(8,128)(2,1)} %reduce-scatter.15.cloned.1.call-done) | copy-start | bytes 7864324
  638.7 2.4 copy-start.2
  642.9 214.3 %reduce-scatter.17.cloned.1.call-start = ((), (), s32[]{:S(2)}) async-start(), calls=%async_computation.21 | async-start | bytes 7864320 | tf_op jit(solution)/shard_map/reduce_scatter | solution.py:213
  730.2 18.1 %slice-start = ((s8[8388608]{0:T(1024)(128)(4,1)}), s8[4194304]{0:T(1024)(128)(4,1)S(1)}, s32[]{:S(2)}) async-start(s8[8388608]{0:T(1024)(128)(4,1)} %bitcast.78), calls=%async_computation.28 | async-start | bytes 8388608
  730.2 23.6 %slice-start.2 = ((s8[5242880]{0:T(1024)(128)(4,1)}), s8[4194304]{0:T(1024)(128)(4,1)S(1)}, s32[]{:S(2)}) async-start(s8[5242880]{0:T(1024)(128)(4,1)} %bitcast.80), calls=%async_computation.30 | async-start | bytes 8388608
  738.3 10.1 slice-start.1
  738.3 15.5 %slice-start.3 = ((s8[5242880]{0:T(1024)(128)(4,1)}), s8[1048576]{0:T(1024)(128)(4,1)S(1)}, s32[]{:S(2)}) async-start(s8[5242880]{0:T(1024)(128)(4,1)} %bitcast.80), calls=%async_computation.31 | async-start | bytes 2097152
  748.4 5.5 copy-start.4
  755.7 3.1 copy-start.6
  760.4 3.4 copy-start.25
  762.1 9.5 copy-start.10
  763.9 7.8 copy-start.11
  763.9 7.8 copy-start.24
  771.7 8.3 copy-start.13
  791.4 138.2 %reduce-scatter.27.cloned.1.call-start = ((), (), s32[]{:S(2)}) async-start(), calls=%async_computation.26 | async-start | bytes 3481600 | tf_op jit(solution)/shard_map/reduce_scatter | solution.py:219
  800.9 198.7 %reduce-scatter.29.cloned.1.call-start = ((), (), s32[]{:S(2)}) async-start(), calls=%async_computation.27 | async-start | bytes 3481600 | tf_op jit(solution)/shard_map/reduce_scatter | solution.py:220
  811.4 9.6 copy-start.16
  811.4 9.6 copy-start.22
  811.4 258.7 %reduce-scatter.25.cloned.1.call-start = ((), (), s32[]{:S(2)}) async-start(), calls=%async_computation.25 | async-start | bytes 3481600 | tf_op jit(solution)/shard_map/reduce_scatter | solution.py:226
  820.7 319.5 %reduce-scatter.19.cloned.1.call-start = ((), (), s32[]{:S(2)}) async-start(), calls=%async_computation.22 | async-start | bytes 3481600 | tf_op jit(solution)/shard_map/reduce_scatter | solution.py:223
  831.1 379.6 %reduce-scatter.21.cloned.1.call-start = ((), (), s32[]{:S(2)}) async-start(), calls=%async_computation.23 | async-start | bytes 3481600 | tf_op jit(solution)/shard_map/reduce_scatter | solution.py:224
  841.0 9.5 copy-start.18
  841.0 10.5 copy-start.28
  841.0 439.7 %reduce-scatter.23.cloned.1.call-start = ((), (), s32[]{:S(2)}) async-start(), calls=%async_computation.24 | async-start | bytes 3481600 | tf_op jit(solution)/shard_map/reduce_scatter | solution.py:225
  857.2 46.1 %copy-start.5 = (bf16[1024,1280]{1,0:T(8,128)(2,1)S(1)}, bf16[1024,1280]{1,0:T(8,128)(2,1)}, u32[]{:S(2)}) copy-start(bf16[1024,1280]{1,0:T(8,128)(2,1)} %reduce-scatter.17.cloned.1.call-done) | copy-start | bytes 7864324
Sparse Core Ops, SparseCore 0:
  10.2 42.6 all-gather.8
  55.0 38.8 all-gather.10
  96.1 38.8 all-gather.12
  136.9 38.8 all-gather.14
  206.9 120.7 reduce-scatter.10
  329.7 39.9 all-gather.18
  371.8 67.4 all-gather.16
  441.4 39.9 all-gather.20
  499.2 64.5 reduce-scatter.14
  566.1 65.6 reduce-scatter.12
  643.0 68.5 all-gather.22
  791.5 65.6 reduce-scatter.16
  862.1 67.4 reduce-scatter.26
  933.8 65.7 reduce-scatter.28
  1004.3 65.7 reduce-scatter.24
  1074.4 65.7 reduce-scatter.18
  1144.9 65.7 reduce-scatter.20
  1214.9 65.7 reduce-scatter.22
where the time goes:
time: 1300 us; the launch traced here: 1290 us
  waiting for transfers between devices  912 us (70%)
  matrix products  195 us (15%)
  local copies, waits for them, and re-layouts  70.2 us (5%)
  other arithmetic  53.2 us (4%)
  blocking collectives  41.1 us (3%)
  between operations  15.2 us (1%)
    reduce_scatter x1, waiting for transfers between devices, shards(): lax.psum_scatter(dot_plain(attended, out_full), 'heads', scatter_dimensio...  113 us
    reduce_scatter x1, waiting for transfers between devices, shards(): lax.psum_scatter(grad_out, 'wide', scatter_dimension=1, tiled=True)  70.6 us
    reduce_scatter x1, waiting for transfers between devices, shards(): lax.psum_scatter(grad_key, 'wide', scatter_dimension=0, tiled=True)  70.5 us
    reduce_scatter x1, waiting for transfers between devices, shards(): lax.psum_scatter(grad_value, 'wide', scatter_dimension=0, tiled=True)  70.1 us
    reduce_scatter x1, waiting for transfers between devices, shards(): lax.psum_scatter(grad_query, 'wide', scatter_dimension=0, tiled=True)  70 us
    reduce_scatter x1, waiting for transfers between devices, shards(): lax.psum_scatter(grad_down, 'wide', scatter_dimension=1, tiled=True)  70 us
    all_gather x1, waiting for transfers between devices, shards(): normed_two = lax.all_gather(normed_half, 'heads', axis=0, tiled=True)  69.6 us
    all_gather x1, waiting for transfers between devices, shards(): grad_branch = lax.all_gather(branch_half, 'heads', axis=0, tiled=True)  68.5 us
  transfers between devices with their start and end apart: 18, of which 17 were waited for; matrix products, arithmetic and copies ran while one was open for 15% of the time, Pallas kernels for 0%

commit v1 on v0

v1 whole, which is shorter than its diff:
```python
import functools
import math

import jax
import jax.numpy as jnp
from jax import lax
from jax.experimental import pallas as pl
from jax.experimental.pallas import tpu as pltpu
from jax.sharding import PartitionSpec as P

DH = 80
PATCHES = 16
EPS = 1e-06
QUERY_BASE = 1.442695041
BF = jnp.bfloat16
F32 = jnp.float32
MESH = pl.DeviceIdType.MESH
ROWS = 256
SEQ = 128
GELU_C = math.sqrt(2.0 / math.pi)


def nn(left, right):
    return jnp.dot(left, right, preferred_element_type=F32)


def nt(left, right):
    return lax.dot_general(left, right, (((1,), (1,)), ((), ())), preferred_element_type=F32)


def tn(left, right):
    return lax.dot_general(left, right, (((0,), (0,)), ((), ())), preferred_element_type=F32)


def inverse_rms(values):
    return lax.rsqrt(jnp.mean(values * values, axis=-1, keepdims=True) + EPS)


def tile(index, size):
    return pl.ds(pl.multiple_of(index * size, size), size)


def head_window(pair):
    return (2 * DH * pair) // 128 * 128


def head_masks(pair):
    lanes = head_window(pair) + lax.broadcasted_iota(jnp.int32, (SEQ, 256), 1)
    picks = []
    for head in (2 * pair, 2 * pair + 1):
        inside = (lanes >= DH * head) & (lanes < DH * (head + 1))
        picks.append(jnp.where(inside, 1.0, 0.0).astype(BF))
    return picks


def block_offset():
    row = lax.broadcasted_iota(jnp.int32, (SEQ, SEQ), 0) // PATCHES
    col = lax.broadcasted_iota(jnp.int32, (SEQ, SEQ), 1) // PATCHES
    return row, col


def roll_rows(values, blocks):
    shift = (blocks % 8) * PATCHES
    if shift == 0:
        return values
    return jnp.concatenate([values[SEQ - shift :], values[: SEQ - shift]], axis=0)


def split_heads(window, masks):
    return jnp.concatenate([window * masks[0], window * masks[1]], axis=0)


def split_rolled(window, masks, slots):
    return jnp.concatenate(
        [roll_rows(window, slots[0]) * masks[0], roll_rows(window, slots[1]) * masks[1]], axis=0
    )


def pack_scores(left_ref, right_ref, rows, group):
    row, col = block_offset()
    offset = lax.rem(row - col + 8, 8)
    packed = jnp.zeros((SEQ, SEQ), F32)
    for pair in range(4 * group, 4 * group + 4):
        win = pl.ds(head_window(pair), 256)
        both = nt(left_ref[rows, win], split_heads(right_ref[rows, win], head_masks(pair)))
        for side in range(2):
            slot = (2 * pair + side) % 8
            one = roll_rows(both[:, SEQ * side : SEQ * (side + 1)], slot)
            packed = jnp.where(offset == slot, one, packed)
    return packed


def spread(packed, group, right_ref, rows):
    row, col = block_offset()
    offset = lax.rem(col - row + 8, 8)
    parts = []
    for pair in range(4 * group, 4 * group + 4):
        slots = (2 * pair % 8, (2 * pair + 1) % 8)
        left = jnp.concatenate(
            [packed * jnp.where(offset == s, 1.0, 0.0).astype(BF) for s in slots], axis=1
        )
        win = pl.ds(head_window(pair), 256)
        parts.append(nn(left, split_rolled(right_ref[rows, win], head_masks(pair), slots)))
    return join_windows(parts)


def join_windows(parts):
    tiles = [parts[0][:, :128]]
    for before, after in zip(parts[:-1], parts[1:]):
        tiles.append(before[:, 128:] + after[:, :128])
    tiles.append(parts[-1][:, 128:])
    return jnp.concatenate(tiles, axis=1)


def softmax_packed(packed, allowed):
    scores = jnp.where(allowed > 0.5, packed, -1e30).reshape(8, PATCHES, SEQ)
    exps = jnp.exp(scores - jnp.max(scores, axis=1, keepdims=True))
    return (exps / jnp.sum(exps, axis=1, keepdims=True)).reshape(SEQ, SEQ)


class Peers:
    def __init__(self):
        wide = lax.axis_index("wide")
        self.y = lax.axis_index("heads")
        self.z = wide // 4
        self.x = lax.rem(wide // 2, 2)
        self.c = lax.rem(wide, 2)

    def device(self, z, x, y, c):
        return ((z * 2 + x) * 2 + c, y)

    def across_x(self):
        return self.device(self.z, 1 - self.x, self.y, self.c)

    def across_y(self):
        return self.device(self.z, self.x, 1 - self.y, self.c)

    def across_core(self):
        return self.device(self.z, self.x, self.y, 1 - self.c)

    def along_z(self, step):
        return self.device(lax.rem(self.z + step, 4), self.x, self.y, self.c)

    def enter(self):
        barrier = pltpu.get_barrier_semaphore()
        others = [self.across_x(), self.across_y(), self.across_core()]
        others += [self.along_z(step) for step in (1, 2, 3)]
        for other in others:
            pl.semaphore_signal(barrier, inc=1, device_id=other, device_id_type=MESH)
        pl.semaphore_wait(barrier, len(others))


class Gather:
    def __init__(self, blocks, full, send_sem, recv_sem, own_sem):
        self.blocks, self.full = blocks, full
        self.send_sem, self.recv_sem, self.own_sem = send_sem, recv_sem, own_sem
        self.peers = Peers()
        self.depth, self.width = blocks[0].shape
        self.sent = [0] * len(blocks)

    def at(self, k, z, x, y, c):
        rows = pl.ds(pl.multiple_of((z * 4 + x * 2 + c) * self.depth, 16), self.depth)
        cols = pl.ds(pl.multiple_of(y * self.width, 128), self.width)
        return self.full.at[k, rows, cols]

    def copy(self, k, place, target, slot, source=None):
        z, x, y, c = place
        there = self.at(k, *place)
        return pltpu.make_async_remote_copy(
            src_ref=there if source is None else source,
            dst_ref=there,
            send_sem=self.send_sem.at[k, slot],
            recv_sem=self.recv_sem.at[k, ((z * 2 + x) * 2 + y) * 2 + c],
            device_id=target,
            device_id_type=MESH,
        )

    def send(self, k, place, target, source=None):
        self.copy(k, place, target, self.sent[k], source).start()
        self.sent[k] += 1

    def arrived(self, k, place):
        self.copy(k, place, self.peers.across_core(), 0).wait_recv()

    def own_copy(self, k):
        p = self.peers
        return pltpu.make_async_copy(self.blocks[k], self.at(k, p.z, p.x, p.y, p.c), self.own_sem.at[k])

    def begin(self):
        p = self.peers
        p.enter()
        own = (p.z, p.x, p.y, p.c)
        for k, block in enumerate(self.blocks):
            for step in (1, 2, 3):
                self.send(k, own, p.along_z(step), block)
            self.send(k, own, p.across_x(), block)
            self.send(k, own, p.across_y(), block)
            self.send(k, own, p.across_core(), block)
            self.own_copy(k).start()

    def from_z(self, k):
        if k >= len(self.blocks):
            return
        p = self.peers
        for step in (1, 3, 2):
            place = (lax.rem(p.z + step, 4), p.x, p.y, p.c)
            self.arrived(k, place)
            for target in (p.across_x(), p.across_y(), p.across_core()):
                self.send(k, place, target)

    def from_plane(self, k):
        if k >= len(self.blocks):
            return
        p = self.peers
        for z in range(4):
            place = (z, 1 - p.x, p.y, p.c)
            self.arrived(k, place)
            if z % 2 == 1:
                self.send(k, place, p.across_y())
            self.send(k, place, p.across_core())
            place = (z, p.x, 1 - p.y, p.c)
            self.arrived(k, place)
            if z % 2 == 0:
                self.send(k, place, p.across_x())
            self.send(k, place, p.across_core())

    def from_corner(self, k):
        p = self.peers
        for z in range(4):
            place = (z, 1 - p.x, 1 - p.y, p.c)
            self.arrived(k, place)
            self.send(k, place, p.across_core())

    def ready(self, k):
        p = self.peers
        self.own_copy(k).wait()
        for z in range(4):
            for x in range(2):
                for y in range(2):
                    self.arrived(k, (z, x, y, 1 - p.c))

    def lead(self):
        self.from_z(0)
        self.from_z(1)
        self.from_plane(0)

    def advance(self, k):
        self.from_z(k + 2)
        self.from_plane(k + 1)
        self.from_corner(k)
        self.ready(k)

    def end(self):
        p = self.peers
        for k in range(len(self.blocks)):
            for slot in range(self.sent[k]):
                self.copy(k, (p.z, p.x, p.y, p.c), p.across_core(), slot).wait_send()


class Loaded:
    def __init__(self, blocks, full, own_sem):
        self.blocks, self.full, self.own_sem = blocks, full, own_sem

    def own_copy(self, k):
        return pltpu.make_async_copy(self.blocks[k], self.full.at[k], self.own_sem.at[k])

    def begin(self):
        for k in range(len(self.blocks)):
            self.own_copy(k).start()

    def lead(self):
        pass

    def advance(self, k):
        self.own_copy(k).wait()

    def end(self):
        pass


def forward_kernel(
    remote,
    x_hbm, g_hbm, allow_ref, vec_ref, w0, w1, w2, w3, w4, w5,
    full_out, n1_out, q_out, k_out, v_out, att_out, n2_out, gp_out, res_out, probs_out, gwd_out, y_out,
    full, xs, n1, qs, ks, vs, att, n2, act, gp, res, probs, gwd,
    own_sem, in_sem, out_sem, *remote_sems,
):
    blocks = (w0, w1, w2, w3, w4, w5)
    tokens = xs.shape[0]
    half = lax.axis_index("heads") * tokens
    x_copy = pltpu.make_async_copy(x_hbm.at[pl.ds(pl.multiple_of(half, 16), tokens)], xs, in_sem.at[0])
    g_copy = pltpu.make_async_copy(g_hbm.at[pl.ds(pl.multiple_of(half, 16), tokens)], xs, in_sem.at[1])
    x_copy.start()
    if remote:
        moves = Gather(blocks, full, *remote_sems, own_sem)
    else:
        moves = Loaded(blocks, full, own_sem)
    moves.begin()
    gain_attn, gain_mlp = vec_ref[0:1], vec_ref[1:2]
    bias_q, bias_v, bias_o = vec_ref[2:3], vec_ref[3:4], vec_ref[4:5]
    bias_up, bias_down, scale = vec_ref[5:6], vec_ref[6:7], vec_ref[7:8]
    stores = []

    def store(source, target):
        copy = pltpu.make_async_copy(source, target, out_sem.at[len(stores)])
        copy.start()
        stores.append(copy)
        return copy

    steps = tokens // ROWS
    x_copy.wait()

    @pl.loop(0, steps)
    def _(i):
        rows = tile(i, ROWS)
        values = xs[rows].astype(F32)
        n1[rows] = (values * inverse_rms(values) * gain_attn).astype(BF)

    store(n1, n1_out)
    moves.lead()
    moves.advance(0)

    @pl.loop(0, steps)
    def _(i):
        rows = tile(i, ROWS)
        qs[rows] = ((nn(n1[rows], full[0]) + bias_q) * scale).astype(BF)

    store(qs, q_out)
    moves.advance(1)

    @pl.loop(0, steps)
    def _(i):
        rows = tile(i, ROWS)
        ks[rows] = nn(n1[rows], full[1]).astype(BF)

    store(ks, k_out)
    moves.advance(2)

    @pl.loop(0, steps)
    def _(i):
        rows = tile(i, ROWS)
        vs[rows] = (nn(n1[rows], full[2]) + bias_v).astype(BF)

    v_store = store(vs, v_out)

    @pl.loop(0, tokens // SEQ)
    def _(i):
        rows = tile(i, SEQ)
        allowed = jnp.concatenate([allow_ref[i]] * 8, axis=0)
        for group in range(2):
            part = softmax_packed(pack_scores(ks, qs, rows, group), allowed)
            probs[i, group] = part.astype(BF)
            att[rows, 640 * group : 640 * (group + 1)] = spread(
                part.T.astype(BF), group, vs, rows
            ).astype(BF)

    store(att, att_out)
    store(probs, probs_out)
    moves.advance(3)

    @pl.loop(0, steps)
    def _(i):
        rows = tile(i, ROWS)
        total = xs[rows].astype(F32) + nt(att[rows], full[3]) + bias_o
        res[rows] = total
        n2[rows] = (total * inverse_rms(total) * gain_mlp).astype(BF)

    g_copy.start()
    store(res, res_out)
    store(n2, n2_out)
    moves.advance(4)

    @pl.loop(0, steps)
    def _(i):
        rows = tile(i, ROWS)
        up = nn(n2[rows], full[4]) + bias_up
        square = up * up
        tanh = jnp.tanh(GELU_C * up * (1.0 + 0.044715 * square))
        act[rows] = (0.5 * up * (1.0 + tanh)).astype(BF)
        slope = 0.5 * (1.0 + tanh) + 0.5 * up * (1.0 - tanh * tanh) * (
            GELU_C * (1.0 + 3 * 0.044715 * square)
        )
        gp[rows] = slope.astype(BF)

    store(gp, gp_out)
    g_copy.wait()

    @pl.loop(0, xs.shape[1] // ROWS)
    def _(i):
        cols = tile(i, ROWS)
        gwd[cols] = tn(xs[:, cols], act[...]).astype(BF)

    store(gwd, gwd_out)
    moves.advance(5)
    if remote:
        for k in range(6):
            store(full.at[k], full_out.at[k])

    v_store.wait()

    @pl.loop(0, steps)
    def _(i):
        rows = tile(i, ROWS)
        vs[rows] = (res[rows] + nt(act[rows], full[5]) + bias_down).astype(BF)

    store(vs, y_out)
    for copy in stores:
        if copy is not v_store:
            copy.wait()
    moves.end()


def forward(remote, tokens, x, g, allow, vecs, weights):
    d = x.shape[1]
    big = jax.ShapeDtypeStruct((tokens, d), BF)
    probs = (tokens // SEQ, 2, SEQ, SEQ)
    outs = [jax.ShapeDtypeStruct((6, d, d), BF)] + [big] * 7 + [
        jax.ShapeDtypeStruct((tokens, d), F32),
        jax.ShapeDtypeStruct(probs, BF),
        jax.ShapeDtypeStruct((d, d), BF),
        big,
    ]
    hbm, vmem = pl.BlockSpec(memory_space=pl.ANY), pl.BlockSpec(memory_space=pltpu.VMEM)
    scratch = [pltpu.VMEM((6, d, d), BF)] + [pltpu.VMEM((tokens, d), BF)] * 9
    scratch += [pltpu.VMEM((tokens, d), F32), pltpu.VMEM(probs, BF), pltpu.VMEM((d, d), BF)]
    scratch += [pltpu.SemaphoreType.DMA((6,)), pltpu.SemaphoreType.DMA((2,)), pltpu.SemaphoreType.DMA((20,))]
    if remote:
        scratch += [pltpu.SemaphoreType.DMA((6, 31)), pltpu.SemaphoreType.DMA((6, 32))]
    return pl.pallas_call(
        functools.partial(forward_kernel, remote),
        out_shape=outs,
        in_specs=[hbm, hbm, vmem, vmem] + [hbm] * 6,
        out_specs=[hbm] * len(outs),
        scratch_shapes=scratch,
        compiler_params=pltpu.CompilerParams(
            collective_id=0 if remote else None,
            has_side_effects=remote,
            vmem_limit_bytes=62 * 2**20,
        ),
        name="forward",
    )(x, g, allow, vecs, *weights)


def norm_back(values, gain_vec, grad_in):
    factor = inverse_rms(values)
    inner = jnp.mean(grad_in * gain_vec * values, axis=-1, keepdims=True)
    grad_out = factor * gain_vec * grad_in - values * factor * factor * factor * inner
    return (grad_out, jnp.sum(grad_in * values * factor, axis=0))


def prepare(inputs, segment_ids, w_out, w_down, b_query, b_value, b_out, b_up, b_down, dim_scale, gain_attn, gain_mlp):
    tokens = inputs.shape[0] // lax.axis_size("heads")
    heads = inputs.shape[1] // DH
    start = lax.axis_index("heads") * tokens
    segs = lax.dynamic_slice_in_dim(segment_ids, start, tokens, 0).reshape(tokens // SEQ, 8, PATCHES)
    place = jnp.arange(PATCHES)
    allow = (segs[:, None, :, :] == segs.transpose(0, 2, 1)[:, :, :, None]) & (
        place[None, :, None, None] <= place[None, None, None, :]
    )
    allow = allow.astype(F32).reshape(tokens // SEQ, PATCHES, SEQ)
    scale = QUERY_BASE / math.sqrt(DH) * jax.nn.softplus(dim_scale)
    vecs = jnp.stack([gain_attn, gain_mlp, b_query, b_value, b_out, b_up, b_down, jnp.tile(scale, heads)])
    return tokens, start, allow, vecs


def shards(
    inputs, segment_ids, cotangent, w_query, w_key, w_value, w_out, w_up, w_down,
    b_query, b_value, b_out, b_up, b_down, dim_scale, gain_attn, gain_mlp,
):
    tokens, start, allow, vecs = prepare(
        inputs, segment_ids, w_out, w_down, b_query, b_value, b_out, b_up, b_down, dim_scale, gain_attn, gain_mlp
    )
    remote = lax.axis_size("wide") == 16 and lax.axis_size("heads") == 2
    weights = [w_query, w_key, w_value, w_out.T, w_up, w_down.T]
    if not remote:
        weights = [
            lax.all_gather(lax.all_gather(w, "heads", axis=1, tiled=True), "wide", axis=0, tiled=True) for w in weights
        ]
    full, n1, qs, ks, vs, att, n2, gp, res, probs, gwd, output = forward(
        remote, tokens, inputs, cotangent, allow, vecs, weights
    )
    if not remote:
        full = jnp.stack(weights)
    g = lax.dynamic_slice_in_dim(cotangent, start, tokens, 0)
    x = lax.dynamic_slice_in_dim(inputs, start, tokens, 0).astype(F32)
    gf = g.astype(F32)
    dup = (nn(g, full[5]) * gp.astype(F32)).astype(BF)
    gwu = tn(n2, dup)
    gn2 = nt(dup, full[4])
    back_two, gg2 = norm_back(res, gain_mlp, gn2)
    gres = gf + back_two
    branch = gres.astype(BF)
    gwo = tn(branch, att)
    gatt = nn(branch, full[3]).astype(BF)
    tc = tokens // SEQ
    nh = w_query.shape[0] * 0 + inputs.shape[1] // DH
    shp = (tc, SEQ, nh, DH)
    q4, k4, v4, g4 = (a.reshape(shp) for a in (qs, ks, vs, gatt))
    q6, k6, v6, g6 = (a.reshape(tc, 8, PATCHES, nh, DH) for a in (q4, k4, v4, g4))
    ok = allow.reshape(tc, PATCHES, 8, PATCHES).transpose(0, 2, 3, 1)[:, None] > 0.5
    sc = jnp.where(ok, jnp.einsum("tbihe,tbjhe->thbij", q6, k6, preferred_element_type=F32), -1e30)
    pk = jax.nn.softmax(sc, axis=-1)
    gpr = jnp.einsum("tbihe,tbjhe->thbij", g6, v6, preferred_element_type=F32)
    inner = jnp.sum(pk * gpr, axis=-1, keepdims=True)
    gs = (pk * (gpr - inner)).astype(BF)
    gq = jnp.einsum("thbij,tbjhe->tbihe", gs, k6, preferred_element_type=F32)
    gk = jnp.einsum("thbij,tbihe->tbjhe", gs, q6, preferred_element_type=F32).reshape(tokens, -1).astype(BF)
    gv = jnp.einsum("thbij,tbihe->tbjhe", pk.astype(BF), g6, preferred_element_type=F32).reshape(tokens, -1).astype(BF)
    scale = vecs[7]
    gq = gq.reshape(tokens, -1)
    gdim = jnp.sum((gq * qs.astype(F32) / scale).reshape(tokens, nh, DH), axis=(0, 1)) * QUERY_BASE / math.sqrt(DH) * jax.nn.sigmoid(dim_scale)
    gq = (gq * scale).astype(BF)
    gw = [tn(n1, gq), tn(n1, gk), tn(n1, gv), gwo, gwu, gwd]
    gn1 = nt(gq, full[0]) + nt(gk, full[1]) + nt(gv, full[2])
    back_one, gg1 = norm_back(x, gain_attn, gn1)
    input_grad = gres + back_one
    def scatter(a):
        a = lax.psum_scatter(a.astype(BF), "wide", scatter_dimension=0, tiled=True)
        return lax.psum_scatter(a, "heads", scatter_dimension=1, tiled=True).astype(F32)
    gw = [scatter(a) for a in gw]
    small = lax.psum((gg1, gg2, jnp.sum(gres, axis=0), jnp.sum(gf, axis=0), gdim, jnp.sum(gq.astype(F32), axis=0), jnp.sum(gv.astype(F32), axis=0), jnp.sum(dup.astype(F32), axis=0)), ("wide", "heads"))
    gg1, gg2, gbo, gbd, gdim, gbq, gbv, gbu = small
    return (output, input_grad, gw[0], gw[1], gw[2], gw[3].T, gw[4], gw[5].T, gbq, gbv, gbo, gbu, gbd, gdim, gg1, gg2)


def solution(mesh):
    token, both = P("wide", None), P(("wide", "heads"), None)
    tall, flat = P("wide", "heads"), P("heads", "wide")
    return jax.shard_map(
        shards,
        mesh=mesh,
        in_specs=(token, P("wide"), token, tall, tall, tall, flat, tall, flat) + (P(),) * 8,
        out_specs=(both, both, tall, tall, tall, flat, tall, flat) + (P(),) * 8,
        check_vma=False,
    )
```

time: 1300 us -> 662 us (0.51)
  waiting for transfers between devices: 912 us -> 207 us
  Pallas kernels: 0 us -> 116 us
  matrix products: 195 us -> 120 us
  local copies, waits for them, and re-layouts: 70.2 us -> 108 us
    reduce_scatter x10 -> x6, waiting for transfers between devices: 605 us -> 130 us  [scatter(): a = lax.psum_scatter(a.astype(BF), 'wide', scatter_dimension=0, tiled=True)]
    all_gather x8 -> x0, waiting for transfers between devices: 303 us -> none  [the longest x1 69.6 us: shards(): normed_two = lax.all_gather(normed_half, 'heads', axis=0, tiled=True)]
    pallas_call x0 -> x1, Pallas kernels: none -> 116 us  [forward(): pl.pallas_call(functools.partial(forward_kernel, remote), out_shape=outs,...]
    dot_general x24 -> x16, matrix products: 195 us -> 120 us  [the longest x4 37.5 us: nt(): lax.dot_general(left, right, (((1,), (1,)), ((), ())), preferred_element_...]
    unnamed x18, waiting for transfers between devices: 4 us -> 77.1 us
    reshape x8 -> x2, local copies, waits for them, and re-layouts: 51.8 us -> 9.18 us  [the longest x1 9.11 us: shards(): gq = gq.reshape(tokens, -1)]
    another operation x3 -> x14, local copies, waits for them, and re-layouts: 0.01 us -> 37.6 us  [the longest x4 32 us: shards(): a.reshape(tc, 8, PATCHES, nh, DH)]
    convert_element_type x4 -> x6, local copies, waits for them, and re-layouts: 6.76 us -> 30.2 us  [the longest x2 10.8 us: shards(): gq = (gq * scale).astype(BF)]
  transfers between devices with their start and end apart: 18 -> 12, of which waited for: 17 -> 9; matrix products, arithmetic and copies ran while one was open for 15% -> 39% of each run, Pallas kernels for 0% -> 0%
where the time goes in v1:
time: 662 us; the launch traced here: 652 us
  waiting for transfers between devices  207 us (31%)
  matrix products  120 us (18%)
  Pallas kernels  116 us (18%)
  local copies, waits for them, and re-layouts  108 us (16%)
  other arithmetic  44.2 us (7%)
  blocking collectives  41.7 us (6%)
  between operations  15.1 us (2%)
    reduce_scatter x6, waiting for transfers between devices, scatter(): a = lax.psum_scatter(a.astype(BF), 'wide', scatter_dimension=0, tiled=True)  130 us
    pallas_call x1, Pallas kernels, forward(): pl.pallas_call(functools.partial(forward_kernel, remote), out_shape=outs,...  116 us
    unnamed x18, waiting for transfers between devices  77.1 us
    psum x1, blocking collectives, shards(): lax.psum((gg1, gg2, jnp.sum(gres, axis=0), jnp.sum(gf, axis=0), gdim, jnp...  41.7 us
    dot_general x4, matrix products, nt(): lax.dot_general(left, right, (((1,), (1,)), ((), ())), preferred_element_...  37.5 us
    dot_general x5, matrix products, tn(): lax.dot_general(left, right, (((0,), (0,)), ((), ())), preferred_element_...  34.8 us
    another operation x4, local copies, waits for them, and re-layouts, shards(): a.reshape(tc, 8, PATCHES, nh, DH)  32 us
    unnamed x57, local copies, waits for them, and re-layouts  21.3 us
  transfers between devices with their start and end apart: 12, of which 9 were waited for; matrix products, arithmetic and copies ran while one was open for 39% of the time, Pallas kernels for 0%

profile of v1, /device:TPU:0, one launch (start us, length us, event | category | flops | bytes accessed | tf_op | source)
XLA Modules:
  0.0 652.2 jit_solution(9344791919344774099)
XLA Ops:
  9.3 0.7 stack.26
  10.0 0.7 stack.27
  10.7 0.7 stack.28
  12.8 0.7 stack.24
  16.3 115.6 %forward.1 = (bf16[6,1280,1280]{2,1,0:T(8,128)(2,1)}, bf16[1024,1280]{1,0:T(8,128)(2,1)}, bf16[1024,1280]{1,0:T(8,128)(2,1)}, bf16[1024,1280]{1,0:T(8,128)(2,1)}...) custom-call(bf16[2048,1280]{1,0:T(8,128)(2,1)} %x_hbm.1, ...), custom_call_target="tpu_custom_call" | custom-call | tf_op jit(solution)/shard_map/forward/pallas_call | solution.py:429
  132.2 7.8 %convert_reduce_fusion.3 = (f32[1280]{0:T(1024)}, bf16[1024,1280]{1,0:T(8,128)(2,1)S(1)}) fusion(bf16[1024,1280]{1,0:T(8,128)(2,1)} %get-tuple-element.30, bf16[6,1280,1280]{2,1,0:T(8,128)(2,1)} %get-tuple-element.29, bf16[2048,1280]{1,0:T(8,128)(2,1)} %g_hbm.1, s32[]{:T(128)S(6)} %select_n.13), kind=kOutput, calls=%fused_computation.33 | convolution fusion | flops 3361995520 | bytes 11146244 | tf_op jit(solution)/shard_map/dot_general | solution.py:24
  140.0 5.0 convolution_convert_fusion
  145.1 3.3 multiply_reduce_fusion.3
  148.4 8.8 %multiply_reduce_fusion.1 = (f32[1280]{0:T(1024)}, f32[1024]{0:T(1024)S(1)}, f32[1024,1280]{1,0:T(8,128)S(1)}) fusion(f32[1024,1280]{1,0:T(8,128)} %get-tuple-element.28, f32[1024]{0:T(1024)S(1)} %add_rsqrt_fusion.1, f32[1280]{0:T(1024)S(1)} %copy-done.11, bf16[1024,1280]{1,0:T(8,128)(2,1)S(1)} %get-tuple-element.63, ...), kind=kOutput, calls=%fused_computation.31 | convolution fusion | flops 3363305216 | bytes 16402432 | tf_op jit(solution)/shard_map/dot_general | solution.py:28
  157.3 2.8 fusion.71
  160.1 2.4 copy-done.1
  162.5 5.1 convolution_convert_fusion.1
  167.6 8.5 %convolution_convert_fusion.5 = bf16[1024,1280]{1,0:T(8,128)(2,1)} fusion(bf16[6,1280,1280]{2,1,0:T(8,128)(2,1)} %get-tuple-element.29, f32[1024,1280]{1,0:T(8,128)} %copy-done.1), kind=kOutput, calls=%fused_computation.58 | convolution fusion | flops 3358064640 | bytes 11141120 | tf_op jit(solution)/shard_map/dot_general | solution.py:24
  176.2 8.9 %reshape_reshape.14 = bf16[8,8,16,16,80]{4,3,2,1,0:T(8,128)(2,1)} reshape(bf16[1024,1280]{1,0:T(8,128)(2,1)} %convolution_convert_fusion.5) | data formatting | bytes 5242880 | tf_op jit(solution)/shard_map/reshape;reshape | solution.py:499
  185.0 7.2 %reshape_reshape.15 = bf16[8,8,16,16,80]{4,3,2,1,0:T(8,128)(2,1)} reshape(bf16[1024,1280]{1,0:T(8,128)(2,1)S(1)} %copy-done.8) | data formatting | bytes 5242880 | tf_op jit(solution)/shard_map/reshape;reshape | solution.py:499
  192.3 9.1 %fusion.25 = f32[8,16,8,16,16]{3,4,2,1,0:T(8,128)} fusion(bf16[8,8,16,16,80]{4,3,2,1,0:T(8,128)(2,1)} %reshape_reshape.15, bf16[8,8,16,16,80]{4,3,2,1,0:T(8,128)(2,1)} %reshape_reshape.14), kind=kOutput, calls=%fused_computation.47 | convolution fusion | flops 41943040 | bytes 6291456 | tf_op jit(solution)/shard_map/tbihe,tbjhe->thbij/dot_general | solution.py:503
  201.6 8.7 %reshape_reshape.12 = bf16[8,8,16,16,80]{4,3,2,1,0:T(8,128)(2,1)} reshape(bf16[1024,1280]{1,0:T(8,128)(2,1)} %get-tuple-element.31) | data formatting | bytes 5242880 | tf_op jit(solution)/shard_map/reshape;reshape | solution.py:499
  210.2 7.2 %reshape_reshape.13 = bf16[8,8,16,16,80]{4,3,2,1,0:T(8,128)(2,1)} reshape(bf16[1024,1280]{1,0:T(8,128)(2,1)S(1)} %copy-done.4) | data formatting | bytes 5242880 | tf_op jit(solution)/shard_map/reshape;reshape | solution.py:499
  217.4 6.1 fusion.28
  223.6 5.7 fusion.72
  229.3 13.6 %multiply_convert_fusion.1 = bf16[8,16,8,16,16]{3,4,2,1,0:T(8,128)(2,1)S(1)} fusion(f32[8,16,8,16,16]{3,4,2,1,0:T(8,128)} %fusion.25, f32[8,16,8,16,16]{3,4,2,1,0:T(8,128)} %get-tuple-element.57, f32[8,16,8,16]{3,2,1,0:T(8,128)S(1)} %get-tuple-element.56), kind=kOutput, calls=%fused_computation.9 | output fusion | flops 1589263 | bytes 2686976 | tf_op jit(solution)/shard_map/sub | solution.py:505
  242.9 2.3 convert_bitcast_fusion.1
  245.2 3.1 copy.86
  248.3 6.6 %convert_element_type.123 = bf16[1024,1280]{1,0:T(8,128)(2,1)S(1)} reshape(bf16[8,8,16,16,80]{4,3,2,1,0:T(8,128)(2,1)} %copy.86) | data formatting | bytes 5242880 | tf_op jit(solution)/shard_map/convert_element_type | solution.py:507
  254.9 8.5 %convolution_convert_fusion.3 = bf16[1280,1280]{1,0:T(8,128)(2,1)} fusion(bf16[1024,1280]{1,0:T(8,128)(2,1)} %get-tuple-element.34, bf16[1024,1280]{1,0:T(8,128)(2,1)S(1)} %convert_element_type.123), kind=kOutput, calls=%fused_computation.16 | convolution fusion | flops 3357081600 | bytes 8519680 | tf_op jit(solution)/shard_map/dot_general | solution.py:32
  263.7 7.0 %convert_reduce_fusion = (f32[16,80]{1,0:T(8,128)S(1)}, bf16[8,8,16,16,80]{4,2,3,1,0:T(8,128)(2,1)S(1)}) fusion(bf16[8,8,16,16,80]{4,3,2,1,0:T(8,128)(2,1)} %reshape_reshape.14, f32[8,16,8,16,16]{3,4,2,1,0:T(8,128)} %get-tuple-element.57, f32[8,16,8,16]{3,2,1,0:T(8,128)S(1)} %get-tuple-element.56), kind=kOutput, calls=%fused_computation.6 | convolution fusion | flops 46398208 | bytes 6362112 | tf_op jit(solution)/shard_map/thbij,tbihe->tbjhe/dot_general | solution.py:508
  270.6 3.1 copy.89
  273.7 6.6 %convert_element_type.127 = bf16[1024,1280]{1,0:T(8,128)(2,1)S(1)} reshape(bf16[8,8,16,16,80]{4,3,2,1,0:T(8,128)(2,1)} %copy.89) | data formatting | bytes 5242880 | tf_op jit(solution)/shard_map/convert_element_type | solution.py:508
  280.3 7.5 %convolution_convert_fusion.2 = bf16[1280,1280]{1,0:T(8,128)(2,1)} fusion(bf16[1024,1280]{1,0:T(8,128)(2,1)} %get-tuple-element.34, bf16[1024,1280]{1,0:T(8,128)(2,1)S(1)} %convert_element_type.127), kind=kOutput, calls=%fused_computation.15 | convolution fusion | flops 3357081600 | bytes 8519680 | tf_op jit(solution)/shard_map/dot_general | solution.py:32
  288.2 6.4 convert_reduce_fusion.1
  294.6 7.3 %copy.90 = f32[8,8,16,16,80]{4,3,2,1,0:T(8,128)} copy(f32[8,8,16,16,80]{4,2,3,1,0:T(8,128)S(1)} %get-tuple-element.58) | data formatting | bytes 10485760 | tf_op jit(solution)/shard_map/thbij,tbjhe->tbihe/transpose | solution.py:506
  301.9 9.1 %reshape.121 = f32[1024,1280]{1,0:T(8,128)} reshape(f32[8,8,16,16,80]{4,3,2,1,0:T(8,128)} %copy.90) | data formatting | bytes 10485760 | tf_op jit(solution)/shard_map/reshape | solution.py:510
  311.0 8.7 %convolution_convert_fusion.4 = bf16[1280,1280]{1,0:T(8,128)(2,1)} fusion(bf16[1024,1280]{1,0:T(8,128)(2,1)} %get-tuple-element.34, f32[1024,1280]{1,0:T(8,128)} %reshape.121, f32[1280]{0:T(1024)S(1)} %mul.200), kind=kOutput, calls=%fused_computation.17 | convolution fusion | flops 3359703040 | bytes 11146240 | tf_op jit(solution)/shard_map/dot_general | solution.py:32
  319.8 1.8 copy.103
  321.9 8.8 %fusion.36 = f32[1024,1280]{1,0:T(8,128)} fusion(bf16[1024,1280]{1,0:T(8,128)(2,1)} %copy-done.7, bf16[6,1280,1280]{2,1,0:T(8,128)(2,1)} %get-tuple-element.29), kind=kOutput, calls=%fused_computation.62 | convolution fusion | flops 3355443200 | bytes 11141120 | tf_op jit(solution)/shard_map/dot_general | solution.py:28
  330.7 3.1 copy.83
  333.8 7.7 %convert_element_type.120 = bf16[1024,1280]{1,0:T(8,128)(2,1)} reshape(bf16[8,8,16,16,80]{4,3,2,1,0:T(8,128)(2,1)} %copy.83) | data formatting | bytes 5242880 | tf_op jit(solution)/shard_map/convert_element_type | solution.py:512
  341.5 1.8 copy.101
  343.4 8.7 %fusion.38 = f32[1024,1280]{1,0:T(8,128)} fusion(bf16[1024,1280]{1,0:T(8,128)(2,1)} %convert_element_type.120, bf16[6,1280,1280]{2,1,0:T(8,128)(2,1)} %get-tuple-element.29), kind=kOutput, calls=%fused_computation.64 | convolution fusion | flops 3355443200 | bytes 11141120 | tf_op jit(solution)/shard_map/dot_general | solution.py:28
  352.1 2.5 fusion.4
  354.6 1.9 copy.99
  356.6 11.3 %fusion.12 = (f32[1280]{0:T(1024)S(1)}, f32[1024]{0:T(1024)S(1)}, f32[1024,1280]{1,0:T(8,128)}) fusion(f32[1024]{0:T(1024)S(1)} %add_rsqrt_fusion, bf16[2048,1280]{1,0:T(8,128)(2,1)} %x_hbm.1, s32[]{:T(128)S(6)} %select_n.13, f32[1280]{0:T(1024)S(1)} %copy-done.12, bf16[1024,1280]{1,0:T(8,128)(2,1)S(1)} %convert_element_type.127, ...), kind=kOutput, calls=%fused_computation.30 | convolution fusion | flops 3367237376 | bytes 24266756 | tf_op jit(solution)/shard_map/dot_general | solution.py:28
  367.9 46.6 %reduce-scatter.27.cloned.1.call-done = bf16[80,1280]{1,0:T(8,128)(2,1)} async-done(((bf16[1280,1280]{1,0:T(8,128)(2,1)}), bf16[80,1280]{1,0:T(8,128)(2,1)}) %reduce-scatter.27.cloned.1.call-update) | async-done | bytes 204816 | tf_op jit(solution)/shard_map/reduce_scatter | solution.py:518
  414.5 1.9 copy.95
  416.5 7.4 %fusion.9 = f32[1024,1280]{1,0:T(8,128)} fusion(f32[1024,1280]{1,0:T(8,128)} %copy-done.1, f32[1024,1280]{1,0:T(8,128)} %get-tuple-element.59, f32[1024]{0:T(1024)S(1)} %broadcast_multiply_fusion, f32[1280]{0:T(1024)S(1)} %copy-done.12, f32[1024]{0:T(1024)S(1)} %add_rsqrt_fusion, bf16[2048,1280]{1,0:T(8,128)(2,1)} %x_hbm.1, s32[]{:T(128)S(6)} %select_n.13), kind=kLoop, calls=%fused_computation.27 | loop fusion | flops 11796480 | bytes 18363396 | tf_op jit(solution)/shard_map/add | solution.py:516
  423.9 60.0 %reduce-scatter.29.cloned.1.call-done = bf16[80,1280]{1,0:T(8,128)(2,1)} async-done(((bf16[1280,1280]{1,0:T(8,128)(2,1)}), bf16[80,1280]{1,0:T(8,128)(2,1)}) %reduce-scatter.29.cloned.1.call-update) | async-done | bytes 204816 | tf_op jit(solution)/shard_map/reduce_scatter | solution.py:518
  483.9 1.8 copy.97
  485.8 3.2 fusion.13
  489.3 41.7 %all-reduce = (f32[1280]{0:T(1024)}, f32[1280]{0:T(1024)}, f32[1280]{0:T(1024)}, f32[1280]{0:T(1024)}, f32[1280]{0:T(1024)}, /*index=5*/f32[80]{0:T(128)}, f32[1280]{0:T(1024)}, f32[1280]{0:T(1024)}) all-reduce(f32[1280]{0:T(1024)S(1)} %reduce_sum.144, ...), channel_id=1, replica_groups=mesh['wide'=16,'heads'=2] {'wide','heads'}, use_global_device_ids=true, to_apply=%region_20.21 | all-reduce | flops 9040 | bytes 72320 | tf_op jit(solution)/shard_map/psum | solution.py:521
  531.1 23.2 %reduce-scatter.25.cloned.1.call-done = bf16[80,1280]{1,0:T(8,128)(2,1)} async-done(((bf16[1280,1280]{1,0:T(8,128)(2,1)}), bf16[80,1280]{1,0:T(8,128)(2,1)}) %reduce-scatter.25.cloned.1.call-update) | async-done | bytes 204816 | tf_op jit(solution)/shard_map/reduce_scatter | solution.py:518
  554.2 1.8 copy.93
  556.1 11.7 %reduce-scatter.47.cloned.1.call-done = bf16[640,80]{1,0:T(8,128)(2,1)} async-done(((bf16[1280,80]{1,0:T(8,128)(2,1)}), bf16[640,80]{1,0:T(8,128)(2,1)}) %reduce-scatter.47.cloned.1.call-update) | async-done | bytes 102416
  567.8 1.0 copy.104
  568.9 13.7 %reduce-scatter.45.cloned.1.call-done = bf16[640,80]{1,0:T(8,128)(2,1)} async-done(((bf16[1280,80]{1,0:T(8,128)(2,1)}), bf16[640,80]{1,0:T(8,128)(2,1)}) %reduce-scatter.45.cloned.1.call-update) | async-done | bytes 102416
  582.6 1.0 copy.102
  584.3 12.9 %reduce-scatter.43.cloned.1.call-done = bf16[640,80]{1,0:T(8,128)(2,1)} async-done(((bf16[1280,80]{1,0:T(8,128)(2,1)}), bf16[640,80]{1,0:T(8,128)(2,1)}) %reduce-scatter.43.cloned.1.call-update) | async-done | bytes 102416
  597.3 1.0 copy.100
  598.3 13.5 %reduce-scatter.39.cloned.1.call-done = bf16[640,80]{1,0:T(8,128)(2,1)} async-done(((bf16[1280,80]{1,0:T(8,128)(2,1)}), bf16[640,80]{1,0:T(8,128)(2,1)}) %reduce-scatter.39.cloned.1.call-update) | async-done | bytes 102416
  611.9 1.0 copy.96
  613.6 12.9 %reduce-scatter.41.cloned.1.call-done = bf16[640,80]{1,0:T(8,128)(2,1)} async-done(((bf16[1280,80]{1,0:T(8,128)(2,1)}), bf16[640,80]{1,0:T(8,128)(2,1)}) %reduce-scatter.41.cloned.1.call-update) | async-done | bytes 102416
  626.5 1.0 copy.98
  629.7 12.0 %reduce-scatter.37.cloned.1.call-done = bf16[640,80]{1,0:T(8,128)(2,1)} async-done(((bf16[1280,80]{1,0:T(8,128)(2,1)}), bf16[640,80]{1,0:T(8,128)(2,1)}) %reduce-scatter.37.cloned.1.call-update) | async-done | bytes 102416
  641.7 1.0 copy.94
  643.5 1.5 copy.146
  (107 shorter events, 12.6 us)
Async XLA Ops:
  7.2 312.6 %reduce-scatter.35.cloned.1.call-start = ((), (), s32[]{:S(2)}) async-start(), calls=%async_computation.17 | async-start | bytes 3481600 | tf_op jit(solution)/shard_map/reduce_scatter | solution.py:518
  132.0 209.5 %reduce-scatter.33.cloned.1.call-start = ((), (), s32[]{:S(2)}) async-start(), calls=%async_computation.16 | async-start | bytes 3481600 | tf_op jit(solution)/shard_map/reduce_scatter | solution.py:518
  132.2 7.8 %copy-start.16 = (bf16[1024,1280]{1,0:T(8,128)(2,1)S(1)}, bf16[1024,1280]{1,0:T(8,128)(2,1)}, u32[]{:S(2)}) copy-start(bf16[1024,1280]{1,0:T(8,128)(2,1)} %get-tuple-element.36) | copy-start | bytes 7864324
  145.0 3.4 copy-start.11
  145.1 209.6 %reduce-scatter.31.cloned.1.call-start = ((), (), s32[]{:S(2)}) async-start(), calls=%async_computation.15 | async-start | bytes 3481600 | tf_op jit(solution)/shard_map/reduce_scatter | solution.py:518
  145.1 12.1 %slice-start = ((s8[5242880]{0:T(1024)(128)(4,1)}), s8[4194304]{0:T(1024)(128)(4,1)S(1)}, s32[]{:S(2)}) async-start(s8[5242880]{0:T(1024)(128)(4,1)} %bitcast.73), calls=%async_computation.24 | async-start | bytes 8388608
  145.1 12.1 %slice-start.2 = ((s8[5242880]{0:T(1024)(128)(4,1)}), s8[4194304]{0:T(1024)(128)(4,1)S(1)}, s32[]{:S(2)}) async-start(s8[5242880]{0:T(1024)(128)(4,1)} %bitcast.75), calls=%async_computation.26 | async-start | bytes 8388608
  148.4 8.8 %slice-start.1 = ((s8[5242880]{0:T(1024)(128)(4,1)}), s8[1048576]{0:T(1024)(128)(4,1)S(1)}, s32[]{:S(2)}) async-start(s8[5242880]{0:T(1024)(128)(4,1)} %bitcast.73), calls=%async_computation.25 | async-start | bytes 2097152
  148.4 8.8 %slice-start.3 = ((s8[5242880]{0:T(1024)(128)(4,1)}), s8[1048576]{0:T(1024)(128)(4,1)S(1)}, s32[]{:S(2)}) async-start(s8[5242880]{0:T(1024)(128)(4,1)} %bitcast.75), calls=%async_computation.27 | async-start | bytes 2097152
  157.2 5.2 copy-start.15
  160.1 2.4 copy-start.1
  167.5 247.0 %reduce-scatter.27.cloned.1.call-start = ((), (), s32[]{:S(2)}) async-start(), calls=%async_computation.13 | async-start | bytes 3481600 | tf_op jit(solution)/shard_map/reduce_scatter | solution.py:518
  176.2 8.9 %copy-start.8 = (bf16[1024,1280]{1,0:T(8,128)(2,1)S(1)}, bf16[1024,1280]{1,0:T(8,128)(2,1)}, u32[]{:S(2)}) copy-start(bf16[1024,1280]{1,0:T(8,128)(2,1)} %get-tuple-element.33) | copy-start | bytes 7864324
  201.4 8.9 %copy-start.4 = (bf16[1024,1280]{1,0:T(8,128)(2,1)S(1)}, bf16[1024,1280]{1,0:T(8,128)(2,1)}, u32[]{:S(2)}) copy-start(bf16[1024,1280]{1,0:T(8,128)(2,1)} %get-tuple-element.32) | copy-start | bytes 7864324
  229.3 13.6 %copy-start = (bf16[8,8,16,16,80]{4,3,2,1,0:T(8,128)(2,1)S(1)}, bf16[8,8,16,16,80]{4,3,2,1,0:T(8,128)(2,1)}, u32[]{:S(2)}) copy-start(bf16[8,8,16,16,80]{4,3,2,1,0:T(8,128)(2,1)} %reshape_reshape.13) | copy-start | bytes 7864324
  242.9 2.3 copy-start.2
  254.9 8.5 %copy-start.7 = (bf16[1024,1280]{1,0:T(8,128)(2,1)}, bf16[1024,1280]{1,0:T(8,128)(2,1)S(1)}, u32[]{:S(2)}) copy-start(bf16[1024,1280]{1,0:T(8,128)(2,1)S(1)} %convert_element_type.123) | copy-start | bytes 7864324
  263.5 220.4 %reduce-scatter.29.cloned.1.call-start = ((), (), s32[]{:S(2)}) async-start(), calls=%async_computation.14 | async-start | bytes 3481600 | tf_op jit(solution)/shard_map/reduce_scatter | solution.py:518
  287.9 266.4 %reduce-scatter.25.cloned.1.call-start = ((), (), s32[]{:S(2)}) async-start(), calls=%async_computation.12 | async-start | bytes 3481600 | tf_op jit(solution)/shard_map/reduce_scatter | solution.py:518
  319.7 248.1 %reduce-scatter.47.cloned.1.call-start = ((), (), s32[]{:S(2)}) async-start(), calls=%async_computation.23 | async-start | bytes 491520
  321.6 261.0 %reduce-scatter.45.cloned.1.call-start = ((), (), s32[]{:S(2)}) async-start(), calls=%async_computation.22 | async-start | bytes 491520
  321.9 8.8 %copy-start.3 = (bf16[8,8,16,16,80]{4,2,3,1,0:T(8,128)(2,1)S(1)}, bf16[8,8,16,16,80]{4,2,3,1,0:T(8,128)(2,1)}, u32[]{:S(2)}) copy-start(bf16[8,8,16,16,80]{4,2,3,1,0:T(8,128)(2,1)} %get-tuple-element.53) | copy-start | bytes 7864324
  343.4 13.2 %copy-start.12 = (f32[1280]{0:T(1024)S(1)}, f32[1280]{0:T(1024)}, u32[]{:S(2)}) copy-start(f32[1280]{0:T(1024)} %param.32) | copy-start | bytes 15364
  343.4 253.9 %reduce-scatter.43.cloned.1.call-start = ((), (), s32[]{:S(2)}) async-start(), calls=%async_computation.21 | async-start | bytes 491520
  356.6 255.3 %reduce-scatter.39.cloned.1.call-start = ((), (), s32[]{:S(2)}) async-start(), calls=%async_computation.19 | async-start | bytes 491520
  416.4 210.2 %reduce-scatter.41.cloned.1.call-start = ((), (), s32[]{:S(2)}) async-start(), calls=%async_computation.20 | async-start | bytes 491520
  416.4 69.4 %copy-start.5 = (bf16[1024,1280]{1,0:T(8,128)(2,1)S(1)}, bf16[1024,1280]{1,0:T(8,128)(2,1)}, u32[]{:S(2)}) copy-start(bf16[1024,1280]{1,0:T(8,128)(2,1)} %get-tuple-element.32) | copy-start | bytes 7864324
  423.8 65.4 %copy-start.17 = (f32[80]{0:T(128)S(1)}, f32[80]{0:T(128)}, u32[]{:S(2)}) copy-start(f32[80]{0:T(128)} %param.31) | copy-start | bytes 964
  423.8 65.5 %copy-start.9 = (f32[1280]{0:T(1024)S(1)}, f32[1280]{0:T(1024)}, u32[]{:S(2)}) copy-start(f32[1280]{0:T(1024)} %get-tuple-element.50) | copy-start | bytes 15364
  423.8 65.5 %copy-start.10 = (f32[1280]{0:T(1024)S(1)}, f32[1280]{0:T(1024)}, u32[]{:S(2)}) copy-start(f32[1280]{0:T(1024)} %get-tuple-element.54) | copy-start | bytes 15364
  423.8 65.5 %copy-start.13 = (f32[1280]{0:T(1024)S(1)}, f32[1280]{0:T(1024)}, u32[]{:S(2)}) copy-start(f32[1280]{0:T(1024)} %get-tuple-element.62) | copy-start | bytes 15364
  423.9 65.5 %copy-start.14 = (f32[1280]{0:T(1024)S(1)}, f32[1280]{0:T(1024)}, u32[]{:S(2)}) copy-start(f32[1280]{0:T(1024)} %get-tuple-element.38) | copy-start | bytes 15364
  485.7 156.0 %reduce-scatter.37.cloned.1.call-start = ((), (), s32[]{:S(2)}) async-start(), calls=%async_computation.18 | async-start | bytes 491520
  489.0 154.4 %copy-start.6 = (bf16[1024,1280]{1,0:T(8,128)(2,1)S(1)}, bf16[1024,1280]{1,0:T(8,128)(2,1)}, u32[]{:S(2)}) copy-start(bf16[1024,1280]{1,0:T(8,128)(2,1)} %get-tuple-element.80) | copy-start | bytes 7864324
Sparse Core Ops, SparseCore 0:
  132.1 72.8 reduce-scatter.34
  209.3 65.6 reduce-scatter.32
  278.9 65.6 reduce-scatter.30
  348.8 65.6 reduce-scatter.26
  418.2 65.6 reduce-scatter.28
  488.0 66.1 reduce-scatter.24
  556.5 11.2 reduce-scatter.46
  570.1 12.3 reduce-scatter.44
  584.8 12.4 reduce-scatter.42
  599.4 12.3 reduce-scatter.38
  614.1 12.4 reduce-scatter.40
  629.3 12.3 reduce-scatter.36

commit v2 on v1

--- a/solution.py
+++ b/solution.py
@@ -441,11 +441,494 @@
     )(x, g, allow, vecs, *weights)
 
 
-def norm_back(values, gain_vec, grad_in):
+ORDER = (5, 4, 3, 2, 0, 1)
+
+
+class Scatter:
+    def __init__(self, grads, pair, first_x, first_y, last_x, last_y, own, far, out, out_vmem, send_sem, recv_sem, credit, out_sem):
+        self.grads, self.pair, self.own, self.far = grads, pair, own, far
+        self.first_x, self.first_y, self.last_x, self.last_y = first_x, first_y, last_x, last_y
+        self.out, self.out_vmem, self.out_sem = out, out_vmem, out_sem
+        self.send_sem, self.recv_sem, self.credit = send_sem, recv_sem, credit
+        self.peers = Peers()
+        self.depth, self.width = own.shape[2:]
+        self.jobs = len(ORDER)
+
+    def begin(self):
+        self.peers.enter()
+
+    def remote(self, j, slot, source, there, target):
+        return pltpu.make_async_remote_copy(
+            src_ref=source,
+            dst_ref=there,
+            send_sem=self.send_sem.at[j, slot],
+            recv_sem=self.recv_sem.at[j, slot],
+            device_id=target,
+            device_id_type=MESH,
+        )
+
+    def grad(self, j):
+        return self.grads.at[j % 2].reshape(8, 2, self.depth, 2 * self.width)
+
+    def half(self, which):
+        return pl.ds(pl.multiple_of(which * self.width, 128), self.width)
+
+    def cores(self, j):
+        return self.remote(j, 0, self.grad(j).at[:, 1 - self.peers.c], self.pair.at[j % 3], self.peers.across_core())
+
+    def outward(self, j):
+        p = self.peers
+        sums = self.pair.at[j % 3]
+        for n in range(2):
+            yield self.remote(j, 1 + n, sums.at[4 * n + 1 - p.x], self.first_x.at[j, n], p.across_x())
+        for n in range(2):
+            yield self.remote(
+                j, 3 + n, sums.at[4 * n + 2 : 4 * n + 4, :, self.half(1 - p.y)], self.first_y.at[j, n], p.across_y()
+            )
+
+    def second(self, j, to_y):
+        p = self.peers
+        if to_y:
+            return self.remote(j, 5, self.first_x.at[j, :, :, self.half(1 - p.y)], self.last_y.at[j], p.across_y())
+        return self.remote(j, 6, self.first_y.at[j, :, 1 - p.x], self.last_x.at[j], p.across_x())
+
+    def depthward(self, j, step):
+        p = self.peers
+        z = lax.rem(p.z + step, 4)
+        return self.remote(j, 6 + step, self.own.at[j, z], self.far.at[j, 3 - step], p.along_z(step))
+
+    def start(self, j):
+        if j >= 3:
+            pl.semaphore_wait(self.credit, 1)
+        self.cores(j).start()
+
+    def pair_sum(self, j):
+        if j < 0 or j >= self.jobs:
+            return
+        p = self.peers
+        self.cores(j).wait_recv()
+        mine, sums = self.grad(j), self.pair.at[j % 3]
+
+        @pl.loop(0, 8)
+        def _(n):
+            sums[n] = (mine[n, p.c].astype(F32) + sums[n].astype(F32)).astype(BF)
+
+        for copy in self.outward(j):
+            copy.start()
+        self.cores(j).wait_send()
+
+    def plane_x(self, j):
+        if j < 0 or j >= self.jobs:
+            return
+        p = self.peers
+        sums = self.pair.at[j % 3]
+        first = list(self.outward(j))
+        for n in range(2):
+            first[n].wait_recv()
+        for n in range(2):
+            self.first_x[j, n] = (self.first_x[j, n].astype(F32) + sums[4 * n + p.x].astype(F32)).astype(BF)
+        self.second(j, True).start()
+
+    def plane_y(self, j):
+        if j < 0 or j >= self.jobs:
+            return
+        p = self.peers
+        sums = self.pair.at[j % 3]
+        first = list(self.outward(j))
+        for n in range(2):
+            first[2 + n].wait_recv()
+        for n in range(2):
+            for x in range(2):
+                total = self.first_y[j, n, x].astype(F32) + sums[4 * n + 2 + x, :, self.half(p.y)].astype(F32)
+                self.first_y[j, n, x] = total.astype(BF)
+        self.second(j, False).start()
+        for copy in first:
+            copy.wait_send()
+        if j + 3 < self.jobs:
+            pl.semaphore_signal(self.credit, inc=1, device_id=p.across_core(), device_id_type=MESH)
+
+    def plane_last(self, j):
+        if j < 0 or j >= self.jobs:
+            return
+        p = self.peers
+        self.second(j, True).wait_recv()
+        for n in range(2):
+            total = self.first_x[j, n, :, self.half(p.y)].astype(F32) + self.last_y[j, n].astype(F32)
+            self.own[j, 2 * n] = total.astype(BF)
+        self.second(j, False).wait_recv()
+        for n in range(2):
+            total = self.first_y[j, n, p.x].astype(F32) + self.last_x[j, n].astype(F32)
+            self.own[j, 2 * n + 1] = total.astype(BF)
+        for step in (2, 1, 3):
+            self.depthward(j, step).start()
+
+    def finish(self, j):
+        if j < 0 or j >= self.jobs:
+            return
+        p = self.peers
+        total = self.own[j, p.z].astype(F32)
+        for step in (1, 2, 3):
+            self.depthward(j, step).wait_recv()
+            total += self.far[j, 3 - step].astype(F32)
+        self.out_vmem[j % 2] = total
+        pltpu.make_async_copy(self.out_vmem.at[j % 2], self.out.at[ORDER[j]], self.out_sem).start()
+        pltpu.make_async_copy(self.out_vmem.at[j % 2], self.out.at[ORDER[j]], self.out_sem).wait()
+
+    def end(self):
+        for j in range(self.jobs):
+            self.second(j, True).wait_send()
+            self.second(j, False).wait_send()
+            for step in (1, 2, 3):
+                self.depthward(j, step).wait_send()
+
+
+class Kept:
+    def __init__(self, grads, out, sems):
+        self.grads, self.out, self.sems = grads, out, sems
+
+    def begin(self):
+        pass
+
+    def copy(self, j):
+        return pltpu.make_async_copy(self.grads.at[j % 2], self.out.at[ORDER[j]], self.sems.at[j])
+
+    def start(self, j):
+        self.copy(j).start()
+        self.copy(j).wait()
+
+    def pair_sum(self, j):
+        pass
+
+    plane_x = plane_y = plane_last = finish = pair_sum
+
+    def end(self):
+        pass
+
+
+class Totals:
+    def __init__(self, sums, got, far, send_sem, recv_sem):
+        self.sums, self.got, self.far, self.send_sem, self.recv_sem = sums, got, far, send_sem, recv_sem
+        self.peers = Peers()
+
+    def copy(self, n, source, there, target):
+        return pltpu.make_async_remote_copy(
+            src_ref=source, dst_ref=there, send_sem=self.send_sem.at[n], recv_sem=self.recv_sem.at[n],
+            device_id=target, device_id_type=MESH,
+        )
+
+    def pair(self, n):
+        target = (self.peers.across_core, self.peers.across_x, self.peers.across_y)[n]()
+        return self.copy(n, self.sums.at[n], self.got.at[n], target)
+
+    def along(self, step):
+        z = self.peers.z
+        return self.copy(2 + step, self.sums.at[3], self.far.at[z], self.peers.along_z(step))
+
+    def coming(self, step):
+        z = lax.rem(self.peers.z - step + 4, 4)
+        return self.copy(2 + step, self.sums.at[3], self.far.at[z], self.peers.along_z(step))
+
+    def start(self, n):
+        if n < 3:
+            self.pair(n).start()
+            return
+        self.far[self.peers.z] = self.sums[3]
+        for step in (1, 2, 3):
+            self.along(step).start()
+
+    def take(self, n):
+        if n < 3:
+            self.pair(n).wait_recv()
+            self.sums[n + 1] = self.sums[n] + self.got[n]
+            return None
+        for step in (1, 2, 3):
+            self.coming(step).wait_recv()
+        return (self.far[0] + self.far[1]) + (self.far[2] + self.far[3])
+
+    def end(self):
+        for n in range(3):
+            self.pair(n).wait_send()
+        for step in (1, 2, 3):
+            self.along(step).wait_send()
+
+
+def gather_back(packed, group, right_ref, rows):
+    row, col = block_offset()
+    diagonal = jnp.where(row == col, 1.0, 0.0).astype(BF)
+    parts = []
+    for pair in range(4 * group, 4 * group + 4):
+        left = jnp.concatenate(
+            [roll_rows(packed, -(2 * pair + side)) * diagonal for side in range(2)], axis=1
+        )
+        win = pl.ds(head_window(pair), 256)
+        parts.append(nn(left, split_heads(right_ref[rows, win], head_masks(pair))))
+    return join_windows(parts)
+
+
+def norm_back(values, gain, grad_in):
     factor = inverse_rms(values)
-    inner = jnp.mean(grad_in * gain_vec * values, axis=-1, keepdims=True)
-    grad_out = factor * gain_vec * grad_in - values * factor * factor * factor * inner
-    return (grad_out, jnp.sum(grad_in * values * factor, axis=0))
+    inner = jnp.mean(grad_in * gain * values, axis=-1, keepdims=True)
+    grad_out = factor * gain * grad_in - values * (factor * factor * factor * inner)
+    return grad_out, jnp.sum(grad_in * values * factor, axis=0, keepdims=True)
+
+
+def add_to(ref, row, cols, values):
+    ref[row : row + 1, cols] = ref[row : row + 1, cols] + values
+
+
+def backward_kernel(
+    remote,
+    x_hbm, g_hbm, vec_ref, full_hbm, n1_hbm, q_hbm, k_hbm, v_hbm, att_hbm, n2_hbm, gp_hbm, res_hbm, probs_hbm, gwd_hbm,
+    in_grad_out, weight_out, sums_out,
+    grads, held, res, gs, ups, n2, att, qs, ks, vs, probs, sums,
+    in_sem, out_sem, *rest,
+):
+    tokens, width = gs.shape
+    half = pl.multiple_of(lax.axis_index("heads") * tokens, 16)
+    count = [0]
+
+    def load(source, target):
+        copy = pltpu.make_async_copy(source, target, in_sem.at[count[0]])
+        count[0] += 1
+        copy.start()
+        return copy
+
+    gwd_in = load(gwd_hbm, grads.at[0])
+    g_in = load(g_hbm.at[pl.ds(half, tokens)], gs)
+    gp_in = load(gp_hbm, ups)
+    down_in = load(full_hbm.at[5], held.at[0])
+    n2_in = load(n2_hbm, n2)
+    up_in = load(full_hbm.at[4], held.at[1])
+    res_in = load(res_hbm, res)
+    att_in = load(att_hbm, att)
+    out_in = load(full_hbm.at[3], held.at[2])
+    v_in = load(v_hbm, vs)
+    q_in = load(q_hbm, qs)
+    k_in = load(k_hbm, ks)
+    probs_in = load(probs_hbm, probs)
+    if remote:
+        moves = Scatter(grads, *rest[:7], weight_out, *rest[7:12])
+        totals = Totals(sums, *rest[12:16])
+    else:
+        moves, totals = Kept(grads, weight_out, rest[0]), None
+    moves.begin()
+    gain_attn, gain_mlp, scale = vec_ref[0:1], vec_ref[1:2], vec_ref[7:8]
+    steps = tokens // ROWS
+    every = slice(None)
+    sums[...] = jnp.zeros_like(sums)
+    small = sums.at[0]
+    gwd_in.wait()
+    moves.start(0)
+    g_in.wait()
+    gp_in.wait()
+    down_in.wait()
+
+    @pl.loop(0, steps)
+    def _(i):
+        rows = tile(i, ROWS)
+        grad_up = (nn(gs[rows], held[0]) * ups[rows].astype(F32)).astype(BF)
+        ups[rows] = grad_up
+        add_to(small, 7, every, jnp.sum(grad_up.astype(F32), axis=0, keepdims=True))
+        add_to(small, 3, every, jnp.sum(gs[rows].astype(F32), axis=0, keepdims=True))
+
+    moves.pair_sum(0)
+    query_in = load(full_hbm.at[0], held.at[0])
+    n2_in.wait()
+
+    @pl.loop(0, width // ROWS)
+    def _(i):
+        cols = tile(i, ROWS)
+        grads[1, cols] = tn(n2[:, cols], ups[...]).astype(BF)
+
+    moves.start(1)
+    up_in.wait()
+    res_in.wait()
+
+    @pl.loop(0, steps)
+    def _(i):
+        rows = tile(i, ROWS)
+        values = res[rows]
+        back, gain_sum = norm_back(values, gain_mlp, nt(ups[rows], held[1]))
+        total = gs[rows].astype(F32) + back
+        res[rows] = total
+        n2[rows] = total.astype(BF)
+        add_to(small, 1, every, gain_sum)
+        add_to(small, 2, every, jnp.sum(total, axis=0, keepdims=True))
+
+    moves.pair_sum(1)
+    key_in = load(full_hbm.at[1], held.at[1])
+    n1_in = load(n1_hbm, ups)
+    att_in.wait()
+
+    @pl.loop(0, width // ROWS)
+    def _(i):
+        cols = tile(i, ROWS)
+        grads[0, cols] = tn(n2[:, cols], att[...]).astype(BF)
+
+    moves.start(2)
+    moves.plane_x(0)
+    moves.plane_y(0)
+    out_in.wait()
+
+    @pl.loop(0, steps)
+    def _(i):
+        rows = tile(i, ROWS)
+        gs[rows] = nn(n2[rows], held[2]).astype(BF)
+
+    value_in = load(full_hbm.at[2], held.at[2])
+    x_in = load(x_hbm.at[pl.ds(half, tokens)], att)
+    moves.pair_sum(2)
+    v_in.wait()
+    q_in.wait()
+    k_in.wait()
+    probs_in.wait()
+
+    def attention(first, last):
+        @pl.loop(first, last)
+        def _(i):
+            rows = tile(i, SEQ)
+            for group in range(2):
+                cols = slice(640 * group, 640 * (group + 1))
+                soft = probs[i, group]
+                grad_soft = pack_scores(vs, gs, rows, group).reshape(8, PATCHES, SEQ)
+                soft_f = soft.astype(F32).reshape(8, PATCHES, SEQ)
+                inner = jnp.sum(soft_f * grad_soft, axis=1, keepdims=True)
+                grad_scores = (soft_f * (grad_soft - inner)).reshape(SEQ, SEQ)
+                by_query = grad_scores.T.astype(BF)
+                by_key = grad_scores.astype(BF)
+                grad_q = spread(by_query, group, ks, rows)
+                grad_k = gather_back(by_key, group, qs, rows).astype(BF)
+                grad_v = gather_back(soft, group, gs, rows).astype(BF)
+                add_to(small, 4, cols, jnp.sum(grad_q * qs[rows, cols].astype(F32), axis=0, keepdims=True))
+                grad_q = (grad_q * scale[:, cols]).astype(BF)
+                add_to(small, 5, cols, jnp.sum(grad_q.astype(F32), axis=0, keepdims=True))
+                add_to(small, 6, cols, jnp.sum(grad_v.astype(F32), axis=0, keepdims=True))
+                qs[rows, cols] = grad_q
+                ks[rows, cols] = grad_k
+                vs[rows, cols] = grad_v
+
+    tiles = tokens // SEQ
+    attention(0, tiles // 4)
+    moves.plane_last(0)
+    moves.plane_x(1)
+    moves.plane_y(1)
+    attention(tiles // 4, tiles // 2)
+    moves.plane_last(1)
+    attention(tiles // 2, 3 * tiles // 4)
+    moves.plane_x(2)
+    moves.plane_y(2)
+    attention(3 * tiles // 4, tiles)
+    moves.finish(0)
+    n1_in.wait()
+
+    def project(slot, values):
+        @pl.loop(0, width // ROWS)
+        def _(i):
+            cols = tile(i, ROWS)
+            grads[slot, cols] = tn(ups[:, cols], values[...]).astype(BF)
+
+    project(1, vs)
+    moves.start(3)
+    moves.plane_last(2)
+    moves.finish(1)
+    project(0, qs)
+    moves.start(4)
+    moves.pair_sum(3)
+    moves.pair_sum(4)
+    project(1, ks)
+    moves.start(5)
+    moves.plane_x(3)
+    moves.plane_y(3)
+    moves.pair_sum(5)
+    moves.finish(2)
+    query_in.wait()
+    key_in.wait()
+    value_in.wait()
+    x_in.wait()
+
+    def enter(first, last):
+        @pl.loop(first, last)
+        def _(i):
+            rows = tile(i, ROWS)
+            grad_norm = nt(qs[rows], held[0]) + nt(ks[rows], held[1]) + nt(vs[rows], held[2])
+            back, gain_sum = norm_back(att[rows].astype(F32), gain_attn, grad_norm)
+            res[rows] = res[rows] + back
+            add_to(small, 0, every, gain_sum)
+
+    enter(0, steps // 2)
+    moves.plane_last(3)
+    moves.plane_x(4)
+    moves.plane_y(4)
+    enter(steps // 2, steps)
+    in_grad = pltpu.make_async_copy(res, in_grad_out, out_sem.at[0])
+    in_grad.start()
+    if remote:
+        totals.start(0)
+    moves.plane_x(5)
+    moves.plane_y(5)
+    if remote:
+        totals.take(0)
+        totals.start(1)
+    moves.plane_last(4)
+    moves.finish(3)
+    if remote:
+        totals.take(1)
+        totals.start(2)
+    moves.plane_last(5)
+    moves.finish(4)
+    if remote:
+        totals.take(2)
+        totals.start(3)
+    moves.finish(5)
+    if remote:
+        sums_out[...] = totals.take(3)
+    else:
+        sums_out[...] = sums[0]
+    in_grad.wait()
+    moves.end()
+    if remote:
+        totals.end()
+
+
+def backward(remote, tokens, x, g, vecs, full, n1, qs, ks, vs, att, n2, gp, res, probs, gwd):
+    d = x.shape[1]
+    hbm, vmem = pl.BlockSpec(memory_space=pl.ANY), pl.BlockSpec(memory_space=pltpu.VMEM)
+    depth, width = (d // lax.axis_size("wide"), d // lax.axis_size("heads")) if remote else (d, d)
+    big = pltpu.VMEM((tokens, d), BF)
+    jobs = len(ORDER)
+    dma, regular = pltpu.SemaphoreType.DMA, pltpu.SemaphoreType.REGULAR
+    scratch = [
+        pltpu.VMEM((2, d, d), BF), pltpu.VMEM((3, d, d), BF), pltpu.VMEM((tokens, d), F32),
+        big, big, big, big, big, big, big, pltpu.VMEM(probs.shape, BF), pltpu.VMEM((4, 8, d), F32),
+        dma((20,)), dma((1,)),
+    ]
+    if remote:
+        block = (depth, width)
+        scratch += [
+            pltpu.VMEM((3, 8, depth, d), BF),
+            pltpu.VMEM((jobs, 2, depth, d), BF), pltpu.VMEM((jobs, 2, 2) + block, BF),
+            pltpu.VMEM((jobs, 2) + block, BF), pltpu.VMEM((jobs, 2) + block, BF),
+            pltpu.VMEM((jobs, 4) + block, BF), pltpu.VMEM((jobs, 3) + block, BF),
+            pltpu.VMEM((2,) + block, F32),
+            dma((jobs, 10)), dma((jobs, 10)), regular, dma,
+            pltpu.VMEM((3, 8, d), F32), pltpu.VMEM((4, 8, d), F32), dma((6,)), dma((6,)),
+        ]
+    else:
+        scratch += [dma((jobs,))]
+    weights = jax.ShapeDtypeStruct((jobs, depth, width), F32 if remote else BF)
+    return pl.pallas_call(
+        functools.partial(backward_kernel, remote),
+        out_shape=[jax.ShapeDtypeStruct((tokens, d), F32), weights, jax.ShapeDtypeStruct((8, d), F32)],
+        in_specs=[hbm, hbm, vmem] + [hbm] * 11,
+        out_specs=[hbm, hbm, vmem],
+        scratch_shapes=scratch,
+        compiler_params=pltpu.CompilerParams(
+            collective_id=1 if remote else None,
+            has_side_effects=remote,
+            vmem_limit_bytes=63 * 2**20,
+        ),
+        name="backward",
+    )(x, g, vecs, full, n1, qs, ks, vs, att, n2, gp, res, probs, gwd)
 
 
 def prepare(inputs, segment_ids, w_out, w_down, b_query, b_value, b_out, b_up, b_down, dim_scale, gain_attn, gain_mlp):
@@ -481,46 +964,19 @@
     )
     if not remote:
         full = jnp.stack(weights)
-    g = lax.dynamic_slice_in_dim(cotangent, start, tokens, 0)
-    x = lax.dynamic_slice_in_dim(inputs, start, tokens, 0).astype(F32)
-    gf = g.astype(F32)
-    dup = (nn(g, full[5]) * gp.astype(F32)).astype(BF)
-    gwu = tn(n2, dup)
-    gn2 = nt(dup, full[4])
-    back_two, gg2 = norm_back(res, gain_mlp, gn2)
-    gres = gf + back_two
-    branch = gres.astype(BF)
-    gwo = tn(branch, att)
-    gatt = nn(branch, full[3]).astype(BF)
-    tc = tokens // SEQ
-    nh = w_query.shape[0] * 0 + inputs.shape[1] // DH
-    shp = (tc, SEQ, nh, DH)
-    q4, k4, v4, g4 = (a.reshape(shp) for a in (qs, ks, vs, gatt))
-    q6, k6, v6, g6 = (a.reshape(tc, 8, PATCHES, nh, DH) for a in (q4, k4, v4, g4))
-    ok = allow.reshape(tc, PATCHES, 8, PATCHES).transpose(0, 2, 3, 1)[:, None] > 0.5
-    sc = jnp.where(ok, jnp.einsum("tbihe,tbjhe->thbij", q6, k6, preferred_element_type=F32), -1e30)
-    pk = jax.nn.softmax(sc, axis=-1)
-    gpr = jnp.einsum("tbihe,tbjhe->thbij", g6, v6, preferred_element_type=F32)
-    inner = jnp.sum(pk * gpr, axis=-1, keepdims=True)
-    gs = (pk * (gpr - inner)).astype(BF)
-    gq = jnp.einsum("thbij,tbjhe->tbihe", gs, k6, preferred_element_type=F32)
-    gk = jnp.einsum("thbij,tbihe->tbjhe", gs, q6, preferred_element_type=F32).reshape(tokens, -1).astype(BF)
-    gv = jnp.einsum("thbij,tbihe->tbjhe", pk.astype(BF), g6, preferred_element_type=F32).reshape(tokens, -1).astype(BF)
-    scale = vecs[7]
-    gq = gq.reshape(tokens, -1)
-    gdim = jnp.sum((gq * qs.astype(F32) / scale).reshape(tokens, nh, DH), axis=(0, 1)) * QUERY_BASE / math.sqrt(DH) * jax.nn.sigmoid(dim_scale)
-    gq = (gq * scale).astype(BF)
-    gw = [tn(n1, gq), tn(n1, gk), tn(n1, gv), gwo, gwu, gwd]
-    gn1 = nt(gq, full[0]) + nt(gk, full[1]) + nt(gv, full[2])
-    back_one, gg1 = norm_back(x, gain_attn, gn1)
-    input_grad = gres + back_one
-    def scatter(a):
-        a = lax.psum_scatter(a.astype(BF), "wide", scatter_dimension=0, tiled=True)
-        return lax.psum_scatter(a, "heads", scatter_dimension=1, tiled=True).astype(F32)
-    gw = [scatter(a) for a in gw]
-    small = lax.psum((gg1, gg2, jnp.sum(gres, axis=0), jnp.sum(gf, axis=0), gdim, jnp.sum(gq.astype(F32), axis=0), jnp.sum(gv.astype(F32), axis=0), jnp.sum(dup.astype(F32), axis=0)), ("wide", "heads"))
-    gg1, gg2, gbo, gbd, gdim, gbq, gbv, gbu = small
-    return (output, input_grad, gw[0], gw[1], gw[2], gw[3].T, gw[4], gw[5].T, gbq, gbv, gbo, gbu, gbd, gdim, gg1, gg2)
+    input_grad, grads, sums = backward(
+        remote, tokens, inputs, cotangent, vecs, full, n1, qs, ks, vs, att, n2, gp, res, probs, gwd
+    )
+    if not remote:
+        grads = lax.psum_scatter(grads, "wide", scatter_dimension=1, tiled=True)
+        grads = lax.psum_scatter(grads, "heads", scatter_dimension=2, tiled=True).astype(F32)
+        sums = lax.psum(sums, ("wide", "heads"))
+    scaled = jnp.sum((sums[4] / vecs[7]).reshape(-1, DH), axis=0)
+    grad_dim = scaled * (QUERY_BASE / math.sqrt(DH)) * jax.nn.sigmoid(dim_scale)
+    return (
+        output, input_grad, grads[0], grads[1], grads[2], grads[3].T, grads[4], grads[5].T,
+        sums[5], sums[6], sums[2], sums[7], sums[3], grad_dim, sums[0], sums[1],
+    )
 
 
 def solution(mesh):

time: 662 us -> 270 us (0.41); the launches traced: 652 us -> 270 us
  waiting for transfers between devices: 207 us -> 0 us
  Pallas kernels: 116 us -> 249 us
  matrix products: 120 us -> 0 us
  local copies, waits for them, and re-layouts: 108 us -> 17.9 us
  other arithmetic: 44.2 us -> 1.88 us
  blocking collectives: 41.7 us -> 0 us
  between operations: 15.1 us -> 0.73 us
    pallas_call x0 -> x1, Pallas kernels: none -> 133 us  [backward(): pl.pallas_call(functools.partial(backward_kernel, remote), out_shape=[jax...]
    reduce_scatter x6 -> x0, waiting for transfers between devices: 130 us -> none  [scatter(): a = lax.psum_scatter(a.astype(BF), 'wide', scatter_dimension=0, tiled=True)]
    dot_general x16 -> x0, matrix products: 120 us -> none  [the longest x4 37.5 us: nt(): lax.dot_general(left, right, (((1,), (1,)), ((), ())), preferred_element_...]
    unnamed x18 -> x0, waiting for transfers between devices: 77.1 us -> none
    psum x1 -> x0, blocking collectives: 41.7 us -> none  [shards(): lax.psum((gg1, gg2, jnp.sum(gres, axis=0), jnp.sum(gf, axis=0), gdim, jnp...]
    another operation x4 -> x0, local copies, waits for them, and re-layouts: 32 us -> none  [shards(): a.reshape(tc, 8, PATCHES, nh, DH)]
    convert_element_type x6 -> x0, local copies, waits for them, and re-layouts: 30.2 us -> none  [the longest x2 10.8 us: shards(): gq = (gq * scale).astype(BF)]
    sub x2 -> x0, other arithmetic: 19.3 us -> none  [the longest x1 13.6 us: shards(): gs = (pk * (gpr - inner)).astype(BF)]
  transfers between devices with their start and end apart: 12 -> 0, of which waited for: 9 -> 0; matrix products, arithmetic and copies ran while one was open for 39% -> 0% of each run, Pallas kernels for 0% -> 0%
where the time goes in v2:
time: 270 us
  Pallas kernels  249 us (92%)
  local copies, waits for them, and re-layouts  17.9 us (7%)
    pallas_call x1, Pallas kernels, backward(): pl.pallas_call(functools.partial(backward_kernel, remote), out_shape=[jax...  133 us
    pallas_call x1, Pallas kernels, forward(): pl.pallas_call(functools.partial(forward_kernel, remote), out_shape=outs,...  116 us
    unnamed x8, local copies, waits for them, and re-layouts  5.8 us
    another operation x9, local copies, waits for them, and re-layouts, prepare(): jnp.stack([gain_attn, gain_mlp, b_query, b_value, b_out, b_up, b_down, jn...  5.67 us

profile of v2, /device:TPU:0, one launch (start us, length us, event | category | flops | bytes accessed | tf_op | source)
XLA Modules:
  0.0 269.5 jit_solution(8079599116451809554)
XLA Ops:
  0.7 0.7 fusion
  1.3 0.7 dynamic-slice_bitcast_fusion
  2.0 0.7 dynamic_slice.3
  2.7 0.7 stack.26
  3.4 0.7 stack.27
  4.1 0.7 stack.28
  4.8 0.7 stack.29
  5.5 0.7 stack.30
  6.2 0.7 stack.24
  6.9 0.7 stack.25
  7.6 0.1 stack_tile.3
  7.7 0.7 stack.31.vec_ref
  8.4 0.1 and.15
  8.5 0.1 reshape.64
  8.6 0.1 copy.33
  8.7 0.2 eq.20
  8.9 0.2 eq.21
  9.1 0.6 and_convert_fusion.allow_ref
  9.7 115.7 %forward.1 = (bf16[6,1280,1280]{2,1,0:T(8,128)(2,1)}, bf16[1024,1280]{1,0:T(8,128)(2,1)}, bf16[1024,1280]{1,0:T(8,128)(2,1)}, bf16[1024,1280]{1,0:T(8,128)(2,1)}...) custom-call(bf16[2048,1280]{1,0:T(8,128)(2,1)} %x_hbm.3, ...), custom_call_target="tpu_custom_call" | custom-call | tf_op jit(solution)/shard_map/forward/pallas_call | solution.py:429
  125.4 0.0 copy-start.2
  125.4 133.3 %backward.1 = (f32[1024,1280]{1,0:T(8,128)}, f32[6,80,640]{2,1,0:T(8,128)}, f32[8,1280]{1,0:T(8,128)}) custom-call(bf16[2048,1280]{1,0:T(8,128)(2,1)} %x_hbm.3, bf16[2048,1280]{1,0:T(8,128)(2,1)} %g_hbm.3, f32[8,1280]{1,0:T(8,128)} %stack.31.vec_ref, bf16[6,1280,1280]{2,1,0:T(8,128)(2,1)} %get-tuple-element.32.full_hbm, ...), custom_call_target="tpu_custom_call" | custom-call | tf_op jit(solution)/shard_map/backward/pallas_call | solution.py:919
  258.7 0.0 copy-start.1
  258.7 2.0 slice_reduce_fusion
  260.7 0.1 squeeze.53
  260.8 0.0 copy-done.2
  260.8 0.5 divide_multiply_fusion
  261.3 2.4 slice_bitcast_fusion
  263.7 0.0 copy-done.1
  263.7 0.0 copy-start
  263.7 1.5 copy.36
  265.2 1.9 copy-done
  267.1 2.4 copy.37
  (4 shorter events, 0.0 us)
Async XLA Ops:
  125.4 135.4 %copy-start.2 = (f32[80]{0:T(128)S(1)}, f32[80]{0:T(128)}, u32[]{:S(2)}) copy-start(f32[80]{0:T(128)} %param.31) | copy-start | bytes 964
  258.7 5.0 %copy-start.1 = (bf16[1024,1280]{1,0:T(8,128)(2,1)S(1)}, bf16[1024,1280]{1,0:T(8,128)(2,1)}, u32[]{:S(2)}) copy-start(bf16[1024,1280]{1,0:T(8,128)(2,1)} %get-tuple-element.76) | copy-start | bytes 7864324
  263.7 3.4 %copy-start = (f32[1024,1280]{1,0:T(8,128)S(1)}, f32[1024,1280]{1,0:T(8,128)}, u32[]{:S(2)}) copy-start(f32[1024,1280]{1,0:T(8,128)} %get-tuple-element.77) | copy-start | bytes 15728644

commit v3 on v1

v3 whole, which is shorter than its diff:
```python
import functools
import math

import jax
import jax.numpy as jnp
from jax import lax
from jax.experimental import pallas as pl
from jax.experimental.pallas import tpu as pltpu
from jax.sharding import PartitionSpec as P

DH = 80
PATCHES = 16
EPS = 1e-06
QUERY_BASE = 1.442695041
BF = jnp.bfloat16
F32 = jnp.float32
MESH = pl.DeviceIdType.MESH
ROWS = 256
SEQ = 128
GELU_C = math.sqrt(2.0 / math.pi)


def nn(left, right):
    return jnp.dot(left, right, preferred_element_type=F32)


def nt(left, right):
    return lax.dot_general(left, right, (((1,), (1,)), ((), ())), preferred_element_type=F32)


def tn(left, right):
    return lax.dot_general(left, right, (((0,), (0,)), ((), ())), preferred_element_type=F32)


def inverse_rms(values):
    return lax.rsqrt(jnp.mean(values * values, axis=-1, keepdims=True) + EPS)


def tile(index, size):
    return pl.ds(pl.multiple_of(index * size, size), size)


def head_window(pair):
    return (2 * DH * pair) // 128 * 128


def head_masks(pair):
    lanes = head_window(pair) + lax.broadcasted_iota(jnp.int32, (SEQ, 256), 1)
    picks = []
    for head in (2 * pair, 2 * pair + 1):
        inside = (lanes >= DH * head) & (lanes < DH * (head + 1))
        picks.append(jnp.where(inside, 1.0, 0.0).astype(BF))
    return picks


def block_offset():
    row = lax.broadcasted_iota(jnp.int32, (SEQ, SEQ), 0) // PATCHES
    col = lax.broadcasted_iota(jnp.int32, (SEQ, SEQ), 1) // PATCHES
    return row, col


def roll_rows(values, blocks):
    shift = (blocks % 8) * PATCHES
    if shift == 0:
        return values
    return jnp.concatenate([values[SEQ - shift :], values[: SEQ - shift]], axis=0)


def split_heads(window, masks):
    return jnp.concatenate([window * masks[0], window * masks[1]], axis=0)


def split_rolled(window, masks, slots):
    return jnp.concatenate(
        [roll_rows(window, slots[0]) * masks[0], roll_rows(window, slots[1]) * masks[1]], axis=0
    )


def pack_scores(left_ref, right_ref, rows, group):
    row, col = block_offset()
    offset = lax.rem(row - col + 8, 8)
    packed = jnp.zeros((SEQ, SEQ), F32)
    for pair in range(4 * group, 4 * group + 4):
        win = pl.ds(head_window(pair), 256)
        both = nt(left_ref[rows, win], split_heads(right_ref[rows, win], head_masks(pair)))
        for side in range(2):
            slot = (2 * pair + side) % 8
            one = roll_rows(both[:, SEQ * side : SEQ * (side + 1)], slot)
            packed = jnp.where(offset == slot, one, packed)
    return packed


def spread(packed, group, right_ref, rows):
    row, col = block_offset()
    offset = lax.rem(col - row + 8, 8)
    parts = []
    for pair in range(4 * group, 4 * group + 4):
        slots = (2 * pair % 8, (2 * pair + 1) % 8)
        left = jnp.concatenate(
            [packed * jnp.where(offset == s, 1.0, 0.0).astype(BF) for s in slots], axis=1
        )
        win = pl.ds(head_window(pair), 256)
        parts.append(nn(left, split_rolled(right_ref[rows, win], head_masks(pair), slots)))
    return join_windows(parts)


def join_windows(parts):
    tiles = [parts[0][:, :128]]
    for before, after in zip(parts[:-1], parts[1:]):
        tiles.append(before[:, 128:] + after[:, :128])
    tiles.append(parts[-1][:, 128:])
    return jnp.concatenate(tiles, axis=1)


def softmax_packed(packed, allowed):
    scores = jnp.where(allowed > 0.5, packed, -1e30).reshape(8, PATCHES, SEQ)
    exps = jnp.exp(scores - jnp.max(scores, axis=1, keepdims=True))
    return (exps / jnp.sum(exps, axis=1, keepdims=True)).reshape(SEQ, SEQ)


class Peers:
    def __init__(self):
        wide = lax.axis_index("wide")
        self.y = lax.axis_index("heads")
        self.z = wide // 4
        self.x = lax.rem(wide // 2, 2)
        self.c = lax.rem(wide, 2)

    def device(self, z, x, y, c):
        return ((z * 2 + x) * 2 + c, y)

    def across_x(self):
        return self.device(self.z, 1 - self.x, self.y, self.c)

    def across_y(self):
        return self.device(self.z, self.x, 1 - self.y, self.c)

    def across_core(self):
        return self.device(self.z, self.x, self.y, 1 - self.c)

    def along_z(self, step):
        return self.device(lax.rem(self.z + step, 4), self.x, self.y, self.c)

    def enter(self):
        barrier = pltpu.get_barrier_semaphore()
        others = [self.across_x(), self.across_y(), self.across_core()]
        others += [self.along_z(step) for step in (1, 2, 3)]
        for other in others:
            pl.semaphore_signal(barrier, inc=1, device_id=other, device_id_type=MESH)
        pl.semaphore_wait(barrier, len(others))


class Gather:
    SLOTS = 37

    def __init__(self, blocks, full, send_sem, recv_sem, own_sem):
        self.blocks, self.full = blocks, full
        self.send_sem, self.recv_sem, self.own_sem = send_sem, recv_sem, own_sem
        self.peers = Peers()
        self.depth, self.width = blocks[0].shape
        self.closed = set()

    def at(self, k, z, x, y, c):
        rows = pl.ds(pl.multiple_of((z * 4 + x * 2 + c) * self.depth, 16), self.depth)
        cols = pl.ds(pl.multiple_of(y * self.width, 128), self.width)
        return self.full.at[k, rows, cols]

    def copy(self, k, place, target, slot, source=None):
        z, x, y, c = place
        there = self.at(k, *place)
        return pltpu.make_async_remote_copy(
            src_ref=there if source is None else source,
            dst_ref=there,
            send_sem=self.send_sem.at[k, slot],
            recv_sem=self.recv_sem.at[k, ((z * 2 + x) * 2 + y) * 2 + c],
            device_id=target,
            device_id_type=MESH,
        )

    def send(self, k, place, target, slot, source=None):
        self.copy(k, place, target, slot, source).start()

    def arrived(self, k, place):
        self.copy(k, place, self.peers.across_core(), 0).wait_recv()

    def own_copy(self, k):
        p = self.peers
        return pltpu.make_async_copy(self.blocks[k], self.at(k, p.z, p.x, p.y, p.c), self.own_sem.at[k])

    def launch(self, k):
        p, block = self.peers, self.blocks[k]
        own = (p.z, p.x, p.y, p.c)
        for side in (1, -1):
            @pl.when(self.inside(p.z + side))
            def _():
                self.send(k, own, p.device(p.z + side, p.x, p.y, p.c), self.z_slot(0, side), block)
        self.send(k, own, p.across_x(), 0, block)
        self.send(k, own, p.across_y(), 1, block)
        self.send(k, own, p.across_core(), 2, block)
        self.own_copy(k).start()

    def inside(self, z):
        return (z >= 0) & (z < 4)

    def z_slot(self, hop, side):
        return 3 + 2 * hop + (1 if side > 0 else 0)

    def from_z(self, k, hop):
        p = self.peers
        for side in (1, -1):
            z = p.z - side * hop
            place = (z, p.x, p.y, p.c)

            @pl.when(self.inside(z))
            def _():
                self.arrived(k, place)
                if hop < 3:
                    @pl.when(self.inside(p.z + side))
                    def _():
                        self.send(k, place, p.device(p.z + side, p.x, p.y, p.c), self.z_slot(hop, side))
                self.send(k, place, p.across_x(), 9 + z)
                self.send(k, place, p.across_y(), 13 + z)
                self.send(k, place, p.across_core(), 17 + z)

    def from_plane(self, k):
        p = self.peers
        for z in range(4):
            place = (z, 1 - p.x, p.y, p.c)
            self.arrived(k, place)
            if z % 2 == 1:
                self.send(k, place, p.across_y(), 29 + z)
            self.send(k, place, p.across_core(), 21 + z)
            place = (z, p.x, 1 - p.y, p.c)
            self.arrived(k, place)
            if z % 2 == 0:
                self.send(k, place, p.across_x(), 29 + z)
            self.send(k, place, p.across_core(), 25 + z)

    def from_corner(self, k):
        p = self.peers
        for z in range(4):
            place = (z, 1 - p.x, 1 - p.y, p.c)
            self.arrived(k, place)
            self.send(k, place, p.across_core(), 33 + z)

    def ready(self, k):
        p = self.peers
        self.own_copy(k).wait()
        for z in range(4):
            for x in range(2):
                for y in range(2):
                    self.arrived(k, (z, x, y, 1 - p.c))

    def close(self, k):
        if k in self.closed:
            return
        self.closed.add(k)
        p = self.peers
        own = (p.z, p.x, p.y, p.c)

        def sent(slot):
            self.copy(k, own, p.across_core(), slot).wait_send()

        for slot in (0, 1, 2) + tuple(range(21, 37)):
            sent(slot)
        for step in (1, 2, 3):
            z = lax.rem(p.z + step, 4)
            for base in (9, 13, 17):
                sent(base + z)
        for hop in range(3):
            for side in (1, -1):
                @pl.when(self.inside(p.z - side * hop) & self.inside(p.z + side))
                def _():
                    sent(self.z_slot(hop, side))


class Loaded:
    def __init__(self, blocks, full, own_sem):
        self.blocks, self.full, self.own_sem = blocks, full, own_sem

    def own_copy(self, k):
        return pltpu.make_async_copy(self.blocks[k], self.full.at[k], self.own_sem.at[k])

    def launch(self, k):
        self.own_copy(k).start()

    def from_z(self, *_):
        pass

    from_plane = from_corner = close = from_z

    def ready(self, k):
        self.own_copy(k).wait()


ORDER = (5, 4, 3, 2, 0, 1)
JOBS = len(ORDER)


class Scatter:
    def __init__(self, full, outs, first_x, first_y, last_x, last_y, own, far, out_vmem, send_sem, recv_sem, credit, out_sem):
        self.full, self.own, self.far, self.outs = full, own, far, outs
        self.first_x, self.first_y, self.last_x, self.last_y = first_x, first_y, last_x, last_y
        self.out_vmem, self.out_sem = out_vmem, out_sem
        self.send_sem, self.recv_sem, self.credit = send_sem, recv_sem, credit
        self.peers = Peers()
        self.depth, self.width = own.shape[2:]
        self.left = [4] * JOBS
        self.sent = set()

    def remote(self, j, slot, source, there, target):
        return pltpu.make_async_remote_copy(
            src_ref=source,
            dst_ref=there,
            send_sem=self.send_sem.at[j, slot],
            recv_sem=self.recv_sem.at[j, slot],
            device_id=target,
            device_id_type=MESH,
        )

    def grad(self, j):
        return self.full.at[j % 2].reshape(8, 2, self.depth, 2 * self.width)

    def pair(self, j):
        return self.full.at[2].reshape(2, 8, self.depth, 2 * self.width).at[j % 2]

    def half(self, which):
        return pl.ds(pl.multiple_of(which * self.width, 128), self.width)

    def cores(self, j):
        return self.remote(j, 0, self.grad(j).at[:, 1 - self.peers.c], self.pair(j), self.peers.across_core())

    def out_x(self, j, n):
        p = self.peers
        return self.remote(j, 1 + n, self.pair(j).at[2 * n + 1 - p.x], self.first_x.at[j, n], p.across_x())

    def out_y(self, j, n):
        p = self.peers
        z = 3 - n
        return self.remote(
            j, 3 + n, self.pair(j).at[2 * z : 2 * z + 2, :, self.half(1 - p.y)], self.first_y.at[j, n], p.across_y()
        )

    def then_y(self, j, n):
        p = self.peers
        return self.remote(j, 5 + n, self.first_x.at[j, n, :, self.half(1 - p.y)], self.last_y.at[j, n], p.across_y())

    def then_x(self, j, n):
        p = self.peers
        return self.remote(j, 7 + n, self.first_y.at[j, n, 1 - p.x], self.last_x.at[j, n], p.across_x())

    def along(self, j, z):
        p = self.peers
        place = lax.rem(p.z - z + 4, 4) - 1
        return self.remote(j, 9 + place, self.own.at[j % 3, z], self.far.at[j, place], p.device(z, p.x, p.y, p.c))

    def open(self):
        pl.semaphore_signal(self.credit, inc=2, device_id=self.peers.across_core(), device_id_type=MESH)

    def start(self, j):
        pl.semaphore_wait(self.credit, 1)
        self.cores(j).start()

    def pair_sum(self, j):
        p = self.peers
        self.cores(j).wait_recv()
        mine, sums = self.grad(j), self.pair(j)

        @pl.loop(0, 8)
        def _(n):
            sums[n] = (mine[n, p.c].astype(F32) + sums[n].astype(F32)).astype(BF)

        for n in range(2):
            self.out_x(j, n).start()
            self.out_y(j, n).start()
        self.cores(j).wait_send()

    def used(self, j):
        self.left[j] -= 1
        if self.left[j] == 0:
            for n in range(2):
                self.out_x(j, n).wait_send()
                self.out_y(j, n).wait_send()
            if j + 2 < JOBS:
                pl.semaphore_signal(self.credit, inc=1, device_id=self.peers.across_core(), device_id_type=MESH)

    def plane_x(self, j, n):
        p = self.peers
        self.out_x(j, n).wait_recv()
        total = self.first_x[j, n].astype(F32) + self.pair(j)[2 * n + p.x].astype(F32)
        self.first_x[j, n] = total.astype(BF)
        self.then_y(j, n).start()
        self.used(j)

    def plane_y(self, j, n):
        p = self.peers
        self.out_y(j, n).wait_recv()
        for x in range(2):
            mine = self.pair(j)[2 * (3 - n) + x, :, self.half(p.y)]
            self.first_y[j, n, x] = (self.first_y[j, n, x].astype(F32) + mine.astype(F32)).astype(BF)
        self.then_x(j, n).start()
        self.used(j)

    def all_sent(self, j):
        if j >= 0 and j not in self.sent:
            self.sent.add(j)
            for step in (1, 2, 3):
                self.along(j, lax.rem(self.peers.z + step, 4)).wait_send()

    def plane_last(self, j, n):
        p = self.peers
        self.all_sent(j - 3)
        self.then_y(j, n).wait_recv()
        total = self.first_x[j, n, :, self.half(p.y)].astype(F32) + self.last_y[j, n].astype(F32)
        self.own[j % 3, n] = total.astype(BF)
        self.then_x(j, n).wait_recv()
        total = self.first_y[j, n, p.x].astype(F32) + self.last_x[j, n].astype(F32)
        self.own[j % 3, 3 - n] = total.astype(BF)
        for z in (n, 3 - n):
            @pl.when(p.z != z)
            def _():
                self.along(j, z).start()

    def out_copy(self, j):
        return pltpu.make_async_copy(self.out_vmem.at[j], self.outs[ORDER[j]], self.out_sem.at[j])

    def finish(self, j):
        p = self.peers
        total = self.own[j % 3, p.z].astype(F32)
        for step in (1, 2, 3):
            self.along(j, lax.rem(p.z + 4 - step, 4)).wait_recv()
        for place in range(3):
            total += self.far[j, place].astype(F32)
        self.out_vmem[j] = total
        self.out_copy(j).start()

    def end(self):
        p = self.peers
        for j in range(JOBS):
            for n in range(2):
                self.then_y(j, n).wait_send()
                self.then_x(j, n).wait_send()
            self.all_sent(j)
            self.out_copy(j).wait()


class Kept:
    def __init__(self, full, outs, sems):
        self.full, self.outs, self.sems = full, outs, sems

    def copy(self, j):
        return pltpu.make_async_copy(self.full.at[j % 2], self.outs[ORDER[j]], self.sems.at[j])

    def start(self, j):
        self.copy(j).start()

    def pair_sum(self, j):
        self.copy(j).wait()

    def open(self, *_):
        pass

    plane_x = plane_y = plane_last = finish = end = open


class Totals:
    def __init__(self, sums, got, far, send_sem, recv_sem):
        self.sums, self.got, self.far, self.send_sem, self.recv_sem = sums, got, far, send_sem, recv_sem
        self.peers = Peers()

    def copy(self, n, source, there, target):
        return pltpu.make_async_remote_copy(
            src_ref=source, dst_ref=there, send_sem=self.send_sem.at[n], recv_sem=self.recv_sem.at[n],
            device_id=target, device_id_type=MESH,
        )

    def pair(self, n):
        target = (self.peers.across_core, self.peers.across_x, self.peers.across_y)[n]()
        return self.copy(n, self.sums.at[n], self.got.at[n], target)

    def along(self, step):
        z = self.peers.z
        return self.copy(2 + step, self.sums.at[3], self.far.at[z], self.peers.along_z(step))

    def coming(self, step):
        z = lax.rem(self.peers.z - step + 4, 4)
        return self.copy(2 + step, self.sums.at[3], self.far.at[z], self.peers.along_z(step))

    def start(self, n):
        if n < 3:
            self.pair(n).start()
            return
        self.far[self.peers.z] = self.sums[3]
        for step in (1, 2, 3):
            self.along(step).start()

    def take(self, n):
        if n < 3:
            self.pair(n).wait_recv()
            self.sums[n + 1] = self.sums[n] + self.got[n]
            return None
        for step in (1, 2, 3):
            self.coming(step).wait_recv()
        return (self.far[0] + self.far[1]) + (self.far[2] + self.far[3])

    def end(self):
        for n in range(3):
            self.pair(n).wait_send()
        for step in (1, 2, 3):
            self.along(step).wait_send()


def gather_back(packed, group, right_ref, rows):
    row, col = block_offset()
    diagonal = jnp.where(row == col, 1.0, 0.0).astype(BF)
    parts = []
    for pair in range(4 * group, 4 * group + 4):
        left = jnp.concatenate(
            [roll_rows(packed, -(2 * pair + side)) * diagonal for side in range(2)], axis=1
        )
        win = pl.ds(head_window(pair), 256)
        parts.append(nn(left, split_heads(right_ref[rows, win], head_masks(pair))))
    return join_windows(parts)


def norm_back(values, gain, grad_in):
    factor = inverse_rms(values)
    inner = jnp.mean(grad_in * gain * values, axis=-1, keepdims=True)
    grad_out = factor * gain * grad_in - values * (factor * factor * factor * inner)
    return grad_out, jnp.sum(grad_in * values * factor, axis=0, keepdims=True)


def allowed_keys(segments):
    query = jnp.broadcast_to(segments.astype(F32), (SEQ, SEQ))
    row, col = block_offset()
    key_at = lax.broadcasted_iota(jnp.int32, (SEQ, SEQ), 0)
    query_at = lax.broadcasted_iota(jnp.int32, (SEQ, SEQ), 1)
    seen = (query.T == query) & (row == col) & (key_at <= query_at)
    return jnp.sum(jnp.where(seen, 1.0, 0.0).reshape(8, PATCHES, SEQ), axis=0)


SCHEDULE = (
    ("launch", 0), ("launch", 1), ("n1", 0, 4), ("launch", 2), ("Z", 0, 1), ("Z", 0, 2), ("Z", 0, 3), ("launch", 3),
    ("Z", 1, 1), ("Z", 1, 2), ("Z", 1, 3), ("launch", 4), ("Z", 2, 1), ("Z", 2, 2), ("Z", 2, 3), ("P", 0), ("P", 1),
    ("C", 0), ("R", 0), ("launch", 5), ("Z", 3, 1), ("q", 0, 4), ("Z", 3, 2), ("Z", 3, 3), ("P", 2), ("C", 1),
    ("R", 1), ("Z", 4, 1), ("k", 0, 4), ("Z", 4, 2), ("Z", 4, 3), ("P", 3), ("C", 2), ("R", 2), ("Z", 5, 1),
    ("v", 0, 4), ("Z", 5, 2), ("af", 0, 3), ("Z", 5, 3), ("P", 4), ("C", 3), ("af", 3, 6), ("R", 3), ("af", 6, 8),
    ("o", 0, 1), ("P", 5), ("o", 1, 4), ("C", 4), ("R", 4), ("u", 0, 3), ("C", 5), ("u", 3, 4), ("gwd", 0, 1),
    ("R", 5), ("gwd", 1, 5), ("s", 0), ("ga", 0, 4), ("p", 0), ("gwu", 0, 5), ("s", 1), ("y", 0, 1), ("X", 0, 0),
    ("Y", 0, 0), ("y", 1, 3), ("p", 1), ("y", 3, 4), ("X", 0, 1), ("Y", 0, 1), ("gn2", 0, 2), ("L", 0, 0),
    ("gn2", 2, 4), ("gwo", 0, 2), ("X", 1, 0), ("Y", 1, 0), ("gwo", 2, 5), ("s", 2), ("gatt", 0, 1), ("X", 1, 1),
    ("Y", 1, 1), ("gatt", 1, 3), ("L", 0, 1), ("p", 2), ("gatt", 3, 4), ("L", 1, 0), ("ab", 0, 2), ("L", 1, 1),
    ("ab", 2, 5), ("F", 0), ("X", 2, 0), ("Y", 2, 0), ("ab", 5, 7), ("X", 2, 1), ("Y", 2, 1), ("ab", 7, 8),
    ("gwv", 0, 1), ("L", 2, 0), ("gwv", 1, 3), ("L", 2, 1), ("F", 1), ("gwv", 3, 5), ("s", 3), ("gwq", 0, 4),
    ("p", 3), ("gwq", 4, 5), ("s", 4), ("gwk", 0, 4), ("p", 4), ("F", 2), ("X", 3, 0), ("Y", 3, 0), ("gwk", 4, 5),
    ("gn1", 0, 1), ("X", 3, 1), ("Y", 3, 1), ("s", 5), ("gn1", 1, 3), ("X", 4, 0), ("Y", 4, 0), ("p", 5),
    ("gn1", 3, 4), ("t", 0), ("X", 4, 1), ("Y", 4, 1), ("L", 3, 0), ("T", 0), ("t", 1), ("L", 3, 1), ("L", 4, 0),
    ("X", 5, 0), ("T", 1), ("t", 2), ("Y", 5, 0), ("X", 5, 1), ("F", 3), ("T", 2), ("t", 3), ("Y", 5, 1),
    ("L", 4, 1), ("L", 5, 0), ("T", 3), ("L", 5, 1), ("F", 4), ("F", 5),
)


def layer_kernel(
    remote,
    x_hbm, g_hbm, seg_ref, dim_ref, gain_attn_in, gain_mlp_in, bias_q_in, bias_v_in, bias_o_in, bias_up_in, bias_down_in,
    w0, w1, w2, w3, w4, w5,
    y_out, in_grad_out, g0, g1, g2, g3, g4, g5,
    s_query, s_value, s_out, s_up, s_down, s_dim, s_gain_attn, s_gain_mlp, spill, n1_spill,
    full, b0, b1, b2, b3, b4, b5, b6, b7, res, probs, sums, vecs,
    own_sem, load_sem, *rest,
):
    tokens, width = b0.shape
    half = pl.multiple_of(lax.axis_index("heads") * tokens, SEQ)
    outs = (g0, g1, g2, g3, g4, g5)
    loads, stores = {}, {}

    def move(name, source, target):
        copy = pltpu.make_async_copy(source, target, load_sem.at[len(loads) + len(stores)])
        copy.start()
        return copy

    def load(name, source, target):
        loads[name] = move(name, source, target)

    def store(name, source, target):
        stores[name] = move(name, source, target)

    def loaded(*names):
        for name in names:
            if name in loads and name not in waited:
                loads[name].wait()
                waited.add(name)

    def stored(*names):
        for name in names:
            if name not in waited:
                stores[name].wait()
                waited.add(name)

    waited = set()
    load("x", x_hbm.at[pl.ds(half, tokens)], b0)
    if remote:
        Peers().enter()
        gather = Gather((w0, w1, w2, w3, w4, w5), full, rest[0], rest[1], own_sem)
        scatter = Scatter(full, outs, *rest[2:13])
        totals = Totals(sums, *rest[13:17])
    else:
        gather = Loaded((w0, w1, w2, w3, w4, w5), full, own_sem)
        scatter, totals = Kept(full, outs, rest[0]), None
    sums[0] = jnp.zeros(sums.shape[1:], F32)
    inputs = (gain_attn_in, gain_mlp_in, bias_q_in, bias_v_in, bias_o_in, bias_up_in, bias_down_in)
    for n, vector in enumerate(inputs):
        vecs[n : n + 1] = vector[...].reshape(1, width)
    factor = QUERY_BASE / math.sqrt(DH)
    dims = dim_ref[...].reshape(1, DH)
    softplus = jnp.maximum(dims, 0.0) + jnp.log(1.0 + jnp.exp(-jnp.abs(dims)))
    vecs[7:8] = jnp.concatenate([factor * softplus] * (width // DH), axis=1)
    gain_attn_ref, gain_mlp_ref, bias_q_ref, bias_v_ref = (vecs.at[n : n + 1] for n in range(4))
    bias_o_ref, bias_up_ref, bias_down_ref, scale_ref = (vecs.at[n : n + 1] for n in range(4, 8))
    small = sums.at[0]
    every = slice(None)

    def add_to(row, cols, values):
        small[row : row + 1, cols] = small[row : row + 1, cols] + values

    def over(first, last, size, body):
        if last - first == 1:
            body(pl.ds(first * size, size), first)
            return

        @pl.loop(first, last)
        def _(i):
            body(tile(i, size), i)

    def normed_one(first, last):
        loaded("x")

        def body(rows, i):
            values = b0[rows].astype(F32)
            b1[rows] = (values * inverse_rms(values) * gain_attn_ref[...]).astype(BF)

        over(first, last, ROWS, body)
        if last * ROWS == tokens:
            store("n1_out", b1, n1_spill)

    def query(first, last):
        def body(rows, i):
            b4[rows] = ((nn(b1[rows], full[0]) + bias_q_ref[...]) * scale_ref[...]).astype(BF)

        over(first, last, ROWS, body)

    def key(first, last):
        def body(rows, i):
            b5[rows] = nn(b1[rows], full[1]).astype(BF)

        over(first, last, ROWS, body)

    def value(first, last):
        def body(rows, i):
            b6[rows] = (nn(b1[rows], full[2]) + bias_v_ref[...]).astype(BF)

        over(first, last, ROWS, body)
        if last * ROWS == tokens:
            if remote:
                stored("w2")
            gather.close(2)
            scatter.open()

    def attend(first, last):
        stored("n1_out")

        def body(rows, i):
            allowed = jnp.concatenate([allowed_keys(seg_ref[pl.ds(lax.axis_index("heads") * (tokens // SEQ) + i, 1)])] * 8, axis=0)
            for group in range(2):
                part = softmax_packed(pack_scores(b5, b4, rows, group), allowed)
                probs[i, group] = part.astype(BF)
                b1[rows, 640 * group : 640 * (group + 1)] = spread(part.T.astype(BF), group, b6, rows).astype(BF)

        over(first, last, SEQ, body)

    def attend_out(first, last):
        def body(rows, i):
            total = b0[rows].astype(F32) + nt(b1[rows], full[3]) + bias_o_ref[...]
            res[rows] = total
            b2[rows] = (total * inverse_rms(total) * gain_mlp_ref[...]).astype(BF)

        over(first, last, ROWS, body)
        if last * ROWS == tokens:
            load("g", g_hbm.at[pl.ds(half, tokens)], b0)

    def up(first, last):
        def body(rows, i):
            up_proj = nn(b2[rows], full[4]) + bias_up_ref[...]
            square = up_proj * up_proj
            tanh = jnp.tanh(GELU_C * up_proj * (1.0 + 0.044715 * square))
            b7[rows] = (0.5 * up_proj * (1.0 + tanh)).astype(BF)
            slope = 0.5 * (1.0 + tanh) + 0.5 * up_proj * (1.0 - tanh * tanh) * (
                GELU_C * (1.0 + 3 * 0.044715 * square)
            )
            b3[rows] = slope.astype(BF)

        over(first, last, ROWS, body)

    def weight_grad(slot, left, right):
        def run(first, last):
            def body(cols, i):
                full[slot, cols] = tn(left[:, cols], right[...]).astype(BF)

            over(first, last, ROWS, body)

        return run

    down_grad = weight_grad(0, b0, b7)

    def grad_down(first, last):
        loaded("g")
        if remote:
            stored("w0")
        gather.close(0)
        down_grad(first, last)

    def down(first, last):
        def body(rows, i):
            b7[rows] = (res[rows] + nt(b7[rows], full[5]) + bias_down_ref[...]).astype(BF)

        over(first, last, ROWS, body)
        rows = pl.ds(first * ROWS, (last - first) * ROWS)
        store(f"y{first}", b7.at[rows], y_out.at[rows])

    def grad_act(first, last):
        def body(rows, i):
            grad_up = (nn(b0[rows], full[5]) * b3[rows].astype(F32)).astype(BF)
            b3[rows] = grad_up
            add_to(7, every, jnp.sum(grad_up.astype(F32), axis=0, keepdims=True))
            add_to(3, every, jnp.sum(b0[rows].astype(F32), axis=0, keepdims=True))

        over(first, last, ROWS, body)

    up_grad = weight_grad(1, b2, b3)

    def grad_up(first, last):
        if remote:
            stored("w1")
        gather.close(1)
        up_grad(first, last)

    def reload(k, slot):
        gather.close(slot)
        load(f"again{k}", spill.at[k] if remote else (w0, w1, w2)[k], full.at[slot])

    def norm_two_back(first, last):
        if first == 0:
            reload(0, 5)

        def body(rows, i):
            back, gain_sum = norm_back(res[rows], gain_mlp_ref[...], nt(b3[rows], full[4]))
            total = b0[rows].astype(F32) + back
            res[rows] = total
            b2[rows] = total.astype(BF)
            add_to(1, every, gain_sum)
            add_to(2, every, jnp.sum(total, axis=0, keepdims=True))

        over(first, last, ROWS, body)
        if last * ROWS == tokens:
            reload(1, 4)
            load("n1", n1_spill, b3)

    grad_out = weight_grad(0, b2, b1)

    def attended_grad(first, last):
        if first == 0:
            load("x2", x_hbm.at[pl.ds(half, tokens)], b1)

        def body(rows, i):
            b0[rows] = nn(b2[rows], full[3]).astype(BF)

        over(first, last, ROWS, body)
        if last * ROWS == tokens:
            reload(2, 3)

    def attend_back(first, last):
        def body(rows, i):
            for group in range(2):
                cols = slice(640 * group, 640 * (group + 1))
                soft = probs[i, group]
                grad_soft = pack_scores(b6, b0, rows, group).reshape(8, PATCHES, SEQ)
                soft_f = soft.astype(F32).reshape(8, PATCHES, SEQ)
                inner = jnp.sum(soft_f * grad_soft, axis=1, keepdims=True)
                grad_scores = (soft_f * (grad_soft - inner)).reshape(SEQ, SEQ)
                grad_q = spread(grad_scores.T.astype(BF), group, b5, rows)
                grad_k = gather_back(grad_scores.astype(BF), group, b4, rows).astype(BF)
                grad_v = gather_back(soft, group, b0, rows).astype(BF)
                add_to(4, cols, jnp.sum(grad_q * b4[rows, cols].astype(F32), axis=0, keepdims=True))
                grad_q = (grad_q * scale_ref[:, cols]).astype(BF)
                add_to(5, cols, jnp.sum(grad_q.astype(F32), axis=0, keepdims=True))
                add_to(6, cols, jnp.sum(grad_v.astype(F32), axis=0, keepdims=True))
                b4[rows, cols] = grad_q
                b5[rows, cols] = grad_k
                b6[rows, cols] = grad_v

        over(first, last, SEQ, body)

    value_grad = weight_grad(1, b3, b6)

    def grad_value(first, last):
        loaded("n1")
        value_grad(first, last)

    def norm_one_back(first, last):
        loaded("again0", "again1", "again2", "x2")

        def body(rows, i):
            grad_norm = nt(b4[rows], full[5]) + nt(b5[rows], full[4]) + nt(b6[rows], full[3])
            back, gain_sum = norm_back(b1[rows].astype(F32), gain_attn_ref[...], grad_norm)
            res[rows] = res[rows] + back
            add_to(0, every, gain_sum)

        over(first, last, ROWS, body)
        rows = pl.ds(first * ROWS, (last - first) * ROWS)
        store(f"dx{first}", res.at[rows], in_grad_out.at[rows])

    def arrived(k):
        gather.ready(k)
        if remote and k < 3:
            store(f"w{k}", full.at[k], spill.at[k])

    def total_start(n):
        if remote:
            totals.start(n)

    def total_take(n):
        done = totals.take(n) if remote else sums[0]
        if n < 3:
            return
        by_lane = done[4:5] / scale_ref[...]
        by_dim = by_lane[:, :DH]
        for head in range(1, width // DH):
            by_dim = by_dim + by_lane[:, DH * head : DH * (head + 1)]
        s_dim[...] = (by_dim * (factor / (1.0 + jnp.exp(-dims)))).reshape(DH)
        rows = ((s_query, 5), (s_value, 6), (s_out, 2), (s_up, 7), (s_down, 3), (s_gain_attn, 0), (s_gain_mlp, 1))
        for target, row in rows:
            target[...] = done[row : row + 1].reshape(width)

    steps = {
        "launch": gather.launch, "Z": gather.from_z, "P": gather.from_plane, "C": gather.from_corner, "R": arrived,
        "n1": normed_one, "q": query, "k": key, "v": value, "af": attend, "o": attend_out, "u": up, "gwd": grad_down,
        "y": down, "ga": grad_act, "gwu": grad_up, "gn2": norm_two_back, "gwo": grad_out, "gatt": attended_grad,
        "ab": attend_back, "gwv": grad_value, "gwq": weight_grad(0, b3, b4), "gwk": weight_grad(1, b3, b5),
        "gn1": norm_one_back, "s": scatter.start, "p": scatter.pair_sum, "X": scatter.plane_x, "Y": scatter.plane_y,
        "L": scatter.plane_last, "F": scatter.finish, "t": total_start, "T": total_take,
    }
    for name, *numbers in SCHEDULE:
        steps[name](*numbers)
    for name, copy in list(stores.items()):
        if name not in waited:
            copy.wait()
    scatter.end()
    if remote:
        totals.end()


def layer(remote, tokens, x, g, segments, vectors, weights):
    d = x.shape[1]
    hbm, vmem = pl.BlockSpec(memory_space=pl.ANY), pl.BlockSpec(memory_space=pltpu.VMEM)
    dma, regular = pltpu.SemaphoreType.DMA, pltpu.SemaphoreType.REGULAR
    big = pltpu.VMEM((tokens, d), BF)
    sums = pltpu.VMEM((4 if remote else 1, 8, d), F32)
    scratch = [pltpu.VMEM((6, d, d), BF)] + [big] * 8
    scratch += [pltpu.VMEM((tokens, d), F32), pltpu.VMEM((tokens // SEQ, 2, SEQ, SEQ), BF), sums, pltpu.VMEM((8, d), F32), dma((6,)), dma((24,))]
    if remote:
        depth, width = d // lax.axis_size("wide"), d // lax.axis_size("heads")
        block = (depth, width)
        scratch += [
            dma((6, Gather.SLOTS)), dma((6, 32)),
            pltpu.VMEM((JOBS, 2, depth, d), BF), pltpu.VMEM((JOBS, 2, 2) + block, BF),
            pltpu.VMEM((JOBS, 2) + block, BF), pltpu.VMEM((JOBS, 2) + block, BF),
            pltpu.VMEM((3, 4) + block, BF), pltpu.VMEM((JOBS, 3) + block, BF),
            pltpu.VMEM((JOBS,) + block, F32),
            dma((JOBS, 12)), dma((JOBS, 12)), regular, dma((JOBS,)),
            pltpu.VMEM((3, 8, d), F32), pltpu.VMEM((4, 8, d), F32), dma((6,)), dma((6,)),
        ]
        grads = [jax.ShapeDtypeStruct(block, F32)] * 6
    else:
        scratch += [dma((JOBS,))]
        grads = [jax.ShapeDtypeStruct((d, d), BF)] * 6
    outs = [
        jax.ShapeDtypeStruct((tokens, d), BF), jax.ShapeDtypeStruct((tokens, d), F32), *grads,
        *[jax.ShapeDtypeStruct((DH if n == 5 else d,), F32) for n in range(8)], jax.ShapeDtypeStruct((3, d, d), BF), jax.ShapeDtypeStruct((tokens, d), BF),
    ]
    return pl.pallas_call(
        functools.partial(layer_kernel, remote),
        out_shape=outs,
        in_specs=[hbm, hbm] + [vmem] * 9 + [hbm] * 6,
        out_specs=[hbm] * 8 + [vmem] * 8 + [hbm] * 2,
        scratch_shapes=scratch,
        compiler_params=pltpu.CompilerParams(
            collective_id=0 if remote else None,
            has_side_effects=remote,
            vmem_limit_bytes=63 * 2**20,
        ),
        name="layer",
    )(x, g, segments, *vectors, *weights)


def shards(
    inputs, segment_ids, cotangent, w_query, w_key, w_value, w_out, w_up, w_down,
    b_query, b_value, b_out, b_up, b_down, dim_scale, gain_attn, gain_mlp,
):
    tokens = inputs.shape[0] // lax.axis_size("heads")
    remote = lax.axis_size("wide") == 16 and lax.axis_size("heads") == 2
    vectors = (dim_scale, gain_attn, gain_mlp, b_query, b_value, b_out, b_up, b_down)
    weights = [w_query, w_key, w_value, w_out.T, w_up, w_down.T]
    if not remote:
        weights = [
            lax.all_gather(lax.all_gather(w, "heads", axis=1, tiled=True), "wide", axis=0, tiled=True) for w in weights
        ]
    output, input_grad, *rest = layer(remote, tokens, inputs, cotangent, segment_ids.reshape(-1, SEQ), vectors, weights)
    grads, sums = rest[:6], rest[6:14]
    if not remote:
        grads = [lax.psum_scatter(grad, "wide", scatter_dimension=0, tiled=True) for grad in grads]
        grads = [lax.psum_scatter(grad, "heads", scatter_dimension=1, tiled=True).astype(F32) for grad in grads]
        sums = lax.psum(sums, ("wide", "heads"))
    grads[3], grads[5] = grads[3].T, grads[5].T
    return (output, input_grad, *grads, *sums)


def solution(mesh):
    token, both = P("wide", None), P(("wide", "heads"), None)
    tall, flat = P("wide", "heads"), P("heads", "wide")
    return jax.shard_map(
        shards,
        mesh=mesh,
        in_specs=(token, P("wide"), token, tall, tall, tall, flat, tall, flat) + (P(),) * 8,
        out_specs=(both, both, tall, tall, tall, flat, tall, flat) + (P(),) * 8,
        check_vma=False,
    )
```

time: 662 us -> 234 us (0.35)
  waiting for transfers between devices: 207 us -> 0 us
  matrix products: 120 us -> 0 us
  Pallas kernels: 116 us -> 213 us
  local copies, waits for them, and re-layouts: 108 us -> 15.1 us
  other arithmetic: 44.2 us -> 0 us
  blocking collectives: 41.7 us -> 0 us
  between operations: 15.1 us -> 0.96 us
    reduce_scatter x6 -> x0, waiting for transfers between devices: 130 us -> none  [scatter(): a = lax.psum_scatter(a.astype(BF), 'wide', scatter_dimension=0, tiled=True)]
    dot_general x16 -> x0, matrix products: 120 us -> none  [the longest x4 37.5 us: nt(): lax.dot_general(left, right, (((1,), (1,)), ((), ())), preferred_element_...]
    pallas_call x1, Pallas kernels: 116 us -> 213 us  [layer(): pl.pallas_call(functools.partial(layer_kernel, remote), out_shape=outs, i...]
    unnamed x18 -> x0, waiting for transfers between devices: 77.1 us -> none
    psum x1 -> x0, blocking collectives: 41.7 us -> none  [shards(): lax.psum((gg1, gg2, jnp.sum(gres, axis=0), jnp.sum(gf, axis=0), gdim, jnp...]
    another operation x14 -> x0, local copies, waits for them, and re-layouts: 37.6 us -> none  [the longest x4 32 us: shards(): a.reshape(tc, 8, PATCHES, nh, DH)]
    convert_element_type x6 -> x0, local copies, waits for them, and re-layouts: 30.2 us -> none  [the longest x2 10.8 us: shards(): gq = (gq * scale).astype(BF)]
    sub x2 -> x0, other arithmetic: 19.3 us -> none  [the longest x1 13.6 us: shards(): gs = (pk * (gpr - inner)).astype(BF)]
  transfers between devices with their start and end apart: 12 -> 0, of which waited for: 9 -> 0; matrix products, arithmetic and copies ran while one was open for 39% -> 0% of each run, Pallas kernels for 0% -> 0%
where the time goes in v3:
time: 234 us; the launch traced here: 229 us
  Pallas kernels  213 us (91%)
  local copies, waits for them, and re-layouts  15.1 us (6%)
    pallas_call x1, Pallas kernels, layer(): pl.pallas_call(functools.partial(layer_kernel, remote), out_shape=outs, i...  213 us
    unnamed x46, local copies, waits for them, and re-layouts  15.1 us

profile of v3, /device:TPU:0, one launch (start us, length us, event | category | flops | bytes accessed | tf_op | source)
XLA Modules:
  0.0 228.9 jit_solution(8132217220709549665)
XLA Ops:
  0.7 212.8 %layer.1 = (bf16[1024,1280]{1,0:T(8,128)(2,1)}, f32[1024,1280]{1,0:T(8,128)}, f32[80,640]{1,0:T(8,128)}, f32[80,640]{1,0:T(8,128)}, f32[80,640]{1,0:T(8,128)}, /...) custom-call(bf16[2048,1280]{1,0:T(8,128)(2,1)} %x_hbm.1, ...), custom_call_target="tpu_custom_call" | custom-call | tf_op jit(solution)/shard_map/layer/pallas_call | solution.py:890
  213.5 0.0 copy-start
  213.5 3.6 %copy.49 = bf16[1024,1280]{1,0:T(8,128)(2,1)} copy(bf16[1024,1280]{1,0:T(8,128)(2,1)} %get-tuple-element.64) | data formatting | bytes 5242880
  217.1 0.4 copy-done
  217.4 0.0 copy-start.6
  217.4 0.0 copy-start.5
  217.4 0.0 copy-start.4
  217.4 0.0 copy-start.3
  217.4 0.0 copy-start.2
  217.4 0.0 copy-start.1
  217.4 0.0 copy-start.13
  217.5 0.0 copy-start.12
  217.5 0.0 copy-start.11
  217.5 0.0 copy-start.10
  217.5 0.0 copy-start.9
  217.5 0.0 copy-start.14
  217.5 0.0 copy-start.8
  217.5 0.0 copy-start.7
  217.5 2.4 %copy.50 = f32[1024,1280]{1,0:T(8,128)} copy(f32[1024,1280]{1,0:T(8,128)S(1)} %copy-done) | data formatting | bytes 10485760
  219.9 0.0 copy-done.6
  219.9 0.7 copy.51
  220.6 0.0 copy-done.5
  220.6 0.7 copy.52
  221.3 0.0 copy-done.4
  221.3 0.7 copy.53
  221.9 0.0 copy-done.3
  221.9 0.7 copy.54
  222.6 0.0 copy-done.2
  222.6 0.7 copy.55
  223.3 0.0 copy-done.1
  223.3 0.7 copy.56
  224.0 0.0 copy-done.13
  224.0 0.6 copy.57
  224.6 0.0 copy-done.12
  224.6 0.6 copy.58
  225.2 0.0 copy-done.11
  225.2 0.6 copy.59
  225.8 0.0 copy-done.10
  225.8 0.6 copy.60
  226.4 0.0 copy-done.9
  226.4 0.6 copy.61
  227.0 0.0 copy-done.14
  227.0 0.5 copy.62
  227.5 0.0 copy-done.8
  227.5 0.6 copy.63
  228.1 0.0 copy-done.7
  228.1 0.6 copy.64
Async XLA Ops:
  213.5 3.9 %copy-start = (f32[1024,1280]{1,0:T(8,128)S(1)}, f32[1024,1280]{1,0:T(8,128)}, u32[]{:S(2)}) copy-start(f32[1024,1280]{1,0:T(8,128)} %get-tuple-element.65) | copy-start | bytes 15728644
  217.4 2.5 %copy-start.6 = (f32[80,640]{1,0:T(8,128)S(1)}, f32[80,640]{1,0:T(8,128)}, u32[]{:S(2)}) copy-start(f32[80,640]{1,0:T(8,128)} %get-tuple-element.66) | copy-start | bytes 614404
  217.4 3.2 %copy-start.5 = (f32[80,640]{1,0:T(8,128)S(1)}, f32[80,640]{1,0:T(8,128)}, u32[]{:S(2)}) copy-start(f32[80,640]{1,0:T(8,128)} %get-tuple-element.67) | copy-start | bytes 614404
  217.4 3.8 %copy-start.4 = (f32[80,640]{1,0:T(8,128)S(1)}, f32[80,640]{1,0:T(8,128)}, u32[]{:S(2)}) copy-start(f32[80,640]{1,0:T(8,128)} %get-tuple-element.68) | copy-start | bytes 614404
  217.4 4.5 %copy-start.3 = (f32[80,640]{1,0:T(8,128)S(1)}, f32[80,640]{1,0:T(8,128)}, u32[]{:S(2)}) copy-start(f32[80,640]{1,0:T(8,128)} %get-tuple-element.37) | copy-start | bytes 614404
  217.4 5.2 %copy-start.2 = (f32[80,640]{1,0:T(8,128)S(1)}, f32[80,640]{1,0:T(8,128)}, u32[]{:S(2)}) copy-start(f32[80,640]{1,0:T(8,128)} %get-tuple-element.70) | copy-start | bytes 614404
  217.4 5.9 %copy-start.1 = (f32[80,640]{1,0:T(8,128)S(1)}, f32[80,640]{1,0:T(8,128)}, u32[]{:S(2)}) copy-start(f32[80,640]{1,0:T(8,128)} %get-tuple-element.39) | copy-start | bytes 614404
  217.4 6.5 %copy-start.13 = (f32[1280]{0:T(1024)S(1)}, f32[1280]{0:T(1024)}, u32[]{:S(2)}) copy-start(f32[1280]{0:T(1024)} %get-tuple-element.72) | copy-start | bytes 15364
  217.5 7.1 %copy-start.12 = (f32[1280]{0:T(1024)S(1)}, f32[1280]{0:T(1024)}, u32[]{:S(2)}) copy-start(f32[1280]{0:T(1024)} %get-tuple-element.73) | copy-start | bytes 15364
  217.5 7.7 %copy-start.11 = (f32[1280]{0:T(1024)S(1)}, f32[1280]{0:T(1024)}, u32[]{:S(2)}) copy-start(f32[1280]{0:T(1024)} %get-tuple-element.74) | copy-start | bytes 15364
  217.5 8.3 %copy-start.10 = (f32[1280]{0:T(1024)S(1)}, f32[1280]{0:T(1024)}, u32[]{:S(2)}) copy-start(f32[1280]{0:T(1024)} %get-tuple-element.75) | copy-start | bytes 15364
  217.5 8.9 %copy-start.9 = (f32[1280]{0:T(1024)S(1)}, f32[1280]{0:T(1024)}, u32[]{:S(2)}) copy-start(f32[1280]{0:T(1024)} %get-tuple-element.76) | copy-start | bytes 15364
  217.5 9.5 %copy-start.14 = (f32[80]{0:T(128)S(1)}, f32[80]{0:T(128)}, u32[]{:S(2)}) copy-start(f32[80]{0:T(128)} %get-tuple-element.77) | copy-start | bytes 964
  217.5 10.0 %copy-start.8 = (f32[1280]{0:T(1024)S(1)}, f32[1280]{0:T(1024)}, u32[]{:S(2)}) copy-start(f32[1280]{0:T(1024)} %get-tuple-element.78) | copy-start | bytes 15364
  217.5 10.6 %copy-start.7 = (f32[1280]{0:T(1024)S(1)}, f32[1280]{0:T(1024)}, u32[]{:S(2)}) copy-start(f32[1280]{0:T(1024)} %get-tuple-element.79) | copy-start | bytes 15364
